TPU v7x, 32 devices: a whole 2x2x4 slice. The times are simulated.
32 devices in a mesh: tm: 4 (over y, core), space: 8 (over z, x).
Axes of the slice: x: 2, y: 2, z: 4, core: 2. Of those that a mesh axis runs over, the one named last changes fastest.
Arguments:
- sources: bfloat16 [4, 2, 4, 3, 12, 8, 128], P('tm', None, None, None, None, 'space'), may hold values from -6 to 6
- gauge_links: bfloat16 [4, 4, 2, 3, 3, 8, 128], P(None, 'tm', None, None, None, 'space'), may hold values from -2.5 to 2.5
- eigenvectors: bfloat16 [4, 128, 2, 3, 8, 128], P('tm', None, None, None, 'space'), may hold values from -0.109375 to 0.109375
- elementals: float32 [4, 2, 128, 128], P('tm', None, 'space'), may hold values from -0.375 to 0.375
Outputs:
- projected: float32 [4, 2, 4, 12, 128], P('tm', None, None, None, 'space')
- contracted: float32 [4, 2, 4, 12, 128], P('tm', None, None, None, 'space')
All inputs are finite; a program needn't handle non-finite values.
Results may differ from a plain program's by a relative error of at most 0.0075.
Values may be sent and summed in bfloat16 or wider, within the bound.
A program may use at most 64 MiB of HBM per device.

v0:
```python
import jax
import jax.numpy as jnp
from jax import lax
from jax.sharding import PartitionSpec as P

LX = 8


highest = lax.Precision.HIGHEST
hopping = 0.125


def with_halo(array, sides, width):
    for axis, dim in sides:
        peers, length = (lax.axis_size(axis), array.shape[dim])
        up = [(i, (i + 1) % peers) for i in range(peers)]
        down = [(j, i) for i, j in up]
        last = lax.slice_in_dim(array, length - width, length, axis=dim)
        leading = lax.slice_in_dim(array, 0, width, axis=dim)
        before = lax.ppermute(last, axis, up)
        after = lax.ppermute(leading, axis, down)
        array = jnp.concatenate([before, array, after], axis=dim)
    return array


def times_unit(value, sign):
    return (-sign * value[1], sign * value[0])


def mult_block(direction, first, second):
    if direction == 0:
        return (times_unit(second, -1.0), times_unit(first, -1.0))
    if direction == 1:
        return ((-second[0], -second[1]), first)
    if direction == 2:
        return (times_unit(first, -1.0), times_unit(second, 1.0))
    return (first, second)


def half_spinor(direction, pair, sign):
    upper_a = (pair[0][:, 0], pair[1][:, 0])
    upper_b = (pair[0][:, 1], pair[1][:, 1])
    lower_a = (pair[0][:, 2], pair[1][:, 2])
    lower_b = (pair[0][:, 3], pair[1][:, 3])
    moved_a, moved_b = mult_block(direction, lower_a, lower_b)
    real_part = jnp.stack([upper_a[0] + sign * moved_a[0], upper_b[0] + sign * moved_b[0]], 1)
    imag_part = jnp.stack([upper_a[1] + sign * moved_a[1], upper_b[1] + sign * moved_b[1]], 1)
    return (real_part, imag_part)


def rebuild(direction, pair, sign):
    first = (pair[0][:, 0], pair[1][:, 0])
    second = (pair[0][:, 1], pair[1][:, 1])
    if direction == 3:
        lower_a = (sign * first[0], sign * first[1])
        lower_b = (sign * second[0], sign * second[1])
    else:
        moved_a, moved_b = mult_block(direction, first, second)
        lower_a = (-sign * moved_a[0], -sign * moved_a[1])
        lower_b = (-sign * moved_b[0], -sign * moved_b[1])
    real_part = jnp.stack([first[0], second[0], lower_a[0], lower_b[0]], 1)
    imag_part = jnp.stack([first[1], second[1], lower_a[1], lower_b[1]], 1)
    return (real_part, imag_part)


def color_apply(link_re, link_im, field_re, field_im, dagger):
    out_re = []
    out_im = []
    for row in range(3):
        acc_re = 0.0
        acc_im = 0.0
        for col in range(3):
            if dagger:
                entry_re = link_re[:, col, row][:, None, None]
                entry_im = -link_im[:, col, row][:, None, None]
            else:
                entry_re = link_re[:, row, col][:, None, None]
                entry_im = link_im[:, row, col][:, None, None]
            vec_re = field_re[:, :, col]
            vec_im = field_im[:, :, col]
            acc_re = acc_re + entry_re * vec_re - entry_im * vec_im
            acc_im = acc_im + entry_re * vec_im + entry_im * vec_re
        out_re.append(acc_re)
        out_im.append(acc_im)
    return (jnp.stack(out_re, 2), jnp.stack(out_im, 2))


def plane_shift(values, direction, stride, row_len):
    if direction == 1:
        return jnp.roll(values, -stride * row_len, axis=-1)
    column = jnp.arange(values.shape[-1]) % row_len
    if stride == 1:
        return jnp.where(
            column == row_len - 1, jnp.roll(values, row_len - 1, -1), jnp.roll(values, -1, -1)
        )
    return jnp.where(column == 0, jnp.roll(values, -(row_len - 1), -1), jnp.roll(values, 1, -1))


def split_parts(values):
    widened = values.astype(jnp.float32)
    return (widened[:, 0], widened[:, 1])


def stored(pair):
    return jnp.stack([pair[0], pair[1]], 1).astype(jnp.bfloat16)


def minus_chi(direction, pair):
    return stored(half_spinor(direction, pair, -1.0))


def plus_chi(direction, pair, link_pair):
    half = half_spinor(direction, pair, 1.0)
    return stored(color_apply(link_pair[0], link_pair[1], half[0], half[1], True))


def direction_term(direction, ahead, behind, link_pair):
    ahead_pair = split_parts(ahead)
    behind_pair = split_parts(behind)
    moved = color_apply(link_pair[0], link_pair[1], ahead_pair[0], ahead_pair[1], False)
    forward = rebuild(direction, moved, -1.0)
    backward = rebuild(direction, behind_pair, 1.0)
    return (forward[0] + backward[0], forward[1] + backward[1])


def contract(matrices, values):

    def product(left, right):
        return jnp.einsum("tkl,tasl->task", left, right, precision=highest)

    real_part = product(matrices[:, 0], values[:, 0]) - product(matrices[:, 1], values[:, 1])
    imag_part = product(matrices[:, 0], values[:, 1]) + product(matrices[:, 1], values[:, 0])
    return jnp.stack([real_part, imag_part], 1)


def local(sources, gauge_links, eigenvectors, elementals):
    tm_last = lax.axis_size("tm") - 1
    tm_index = lax.axis_index("tm")
    local_t = sources.shape[0]
    link_here = [split_parts(gauge_links[direction]) for direction in range(4)]
    tpos = jnp.arange(local_t).reshape(-1, 1, 1, 1, 1, 1, 1)
    ahead_sign = jnp.where((tpos == local_t - 1) & (tm_index == tm_last), -1.0, 1.0)
    behind_sign = jnp.where((tpos == 0) & (tm_index == 0), -1.0, 1.0)
    current = sources
    for sweep in range(3):
        pair = split_parts(current)
        ahead = {}
        behind = {}
        for apply_direction in range(2):
            ahead[apply_direction] = plane_shift(
                minus_chi(apply_direction, pair), apply_direction, 1, LX
            )
            behind[apply_direction] = plane_shift(
                plus_chi(apply_direction, pair, link_here[apply_direction]), apply_direction, -1, LX
            )
        minus_t = minus_chi(3, pair)
        plus_t = plus_chi(3, pair, link_here[3])
        rim_t = jnp.concatenate([minus_t, plus_t], 0)
        padded_t = with_halo(rim_t, (("tm", 0),), 1)
        ahead[3] = ahead_sign * jnp.concatenate([minus_t[1:], padded_t[-1:]], 0).astype(jnp.float32)
        behind[3] = behind_sign * jnp.concatenate([padded_t[:1], plus_t[:-1]], 0).astype(
            jnp.float32
        )
        minus_z = minus_chi(2, pair)
        plus_z = plus_chi(2, pair, link_here[2])
        rim_z = jnp.concatenate([minus_z, plus_z], 5)
        padded_z = with_halo(rim_z, (("space", 5),), 1)
        ahead[2] = jnp.concatenate(
            [minus_z[:, :, :, :, :, 1:, :], padded_z[:, :, :, :, :, -1:, :]], 5
        )
        behind[2] = jnp.concatenate(
            [padded_z[:, :, :, :, :, :1, :], plus_z[:, :, :, :, :, :-1, :]], 5
        )
        result_re = 0.0
        result_im = 0.0
        for apply_direction in range(4):
            term_re, term_im = direction_term(
                apply_direction,
                ahead[apply_direction],
                behind[apply_direction],
                link_here[apply_direction],
            )
            result_re = result_re + term_re
            result_im = result_im + term_im
        current = (
            sources.astype(jnp.float32) + hopping * jnp.stack([result_re, result_im], 1)
        ).astype(jnp.bfloat16)
    flipped = jnp.stack([current[:, 1], -current[:, 0]], 1)
    stacked = jnp.stack([current, flipped], 1)
    partial_value = jnp.einsum(
        "tkrczp,toracszp->toask", eigenvectors, stacked, preferred_element_type=jnp.float32
    )
    modes_dev = elementals.shape[2]
    totals = lax.psum(partial_value, "space")
    projected = lax.dynamic_slice_in_dim(totals, lax.axis_index("space") * modes_dev, modes_dev, 4)
    contracted = contract(elementals, totals)
    return (projected, contracted)


def solution(mesh):
    placed = (
        P("tm", None, None, None, None, "space", None),
        P(None, "tm", None, None, None, "space", None),
        P("tm", None, None, None, "space", None),
        P("tm", None, "space", None),
    )
    return jax.shard_map(
        local,
        mesh=mesh,
        in_specs=placed,
        out_specs=(P("tm", None, None, None, "space"), P("tm", None, None, None, "space")),
        check_vma=False,
    )
```

profile of v0, /device:TPU:0, one launch (start us, length us, event | category | flops | bytes accessed | tf_op | source)
XLA Modules:
  0.0 75.7 jit_solution(203832238984547237)
XLA Ops:
  0.6 0.0 copy-start
  0.6 0.9 %copy_convert_fusion = f32[1,2,4,3,12,1,128]{6,4,3,2,5,1,0:T(8,128)S(1)} fusion(bf16[1,2,4,3,12,1,128]{6,2,5,4,3,1,0:T(4,128)(2,1)} %param.4), kind=kLoop, calls=%fused_computation.76 | loop fusion | flops 36864 | bytes 221184 | tf_op jit(solution)/shard_map/convert_element_type | solution.py:186
  1.7 0.0 copy-start.3
  1.7 0.7 copy-done.3
  2.6 0.5 collective-permute-start.3
  3.3 2.6 %collective-permute-start.1 = (bf16[1,2,2,3,12,1,128]{6,4,3,2,5,1,0:T(8,128)(2,1)S(1)}, bf16[1,2,2,3,12,1,128]{6,4,3,2,5,1,0:T(8,128)(2,1)S(1)}, u32[]{:S(2)}, u32[]{:S(2)}) collective-permute-start(bf16[1,2,2,3,12,1,128]{6,4,3,2,5,1,0:T(8,128)(2,1)S(1)} %pad_maximum_fusion.24), channel_id=1, source_target_pairs={{0,1},{1,2},{2,3},{3,4},{4,5},{5,6},{6,7},{7,0},{8,9},{9,10},{10,1... | collective-permute-start | bytes 110600 | tf_op jit(solution)/shard_map/ppermute | solution.py:20
  6.0 3.1 %collective-permute-start = (bf16[1,2,2,3,12,1,128]{6,4,3,2,5,1,0:T(8,128)(2,1)S(1)}, bf16[1,2,2,3,12,1,128]{6,4,3,2,5,1,0:T(8,128)(2,1)S(1)}, u32[]{:S(2)}, u32[]{:S(2)}) collective-permute-start(bf16[1,2,2,3,12,1,128]{6,4,3,2,5,1,0:T(8,128)(2,1)S(1)} %pad_maximum_fusion.21), channel_id=1, source_target_pairs={{1,0},{2,1},{3,2},{4,3},{5,4},{6,5},{7,6},{0,7},{9,8},{10,9},{11,1... | collective-permute-start | bytes 110600 | tf_op jit(solution)/shard_map/ppermute | solution.py:21
  9.1 1.5 %collective-permute-start.2 = (bf16[1,2,2,3,12,1,128]{6,4,3,2,5,1,0:T(8,128)(2,1)S(1)}, bf16[1,2,2,3,12,1,128]{6,4,3,2,5,1,0:T(8,128)(2,1)S(1)}, u32[]{:S(2)}, u32[]{:S(2)}) collective-permute-start(bf16[1,2,2,3,12,1,128]{6,4,3,2,5,1,0:T(8,128)(2,1)S(1)} %pad_maximum_fusion.25), channel_id=1, source_target_pairs={{8,0},{16,8},{24,16},{0,24},{9,1},{17,9},{25,17},{1,25},{10,2},{18... | collective-permute-start | bytes 110600 | tf_op jit(solution)/shard_map/ppermute | solution.py:21
  10.9 0.1 fusion.52
  11.0 0.1 fusion.53
  11.1 0.1 fusion.55
  11.2 0.1 fusion.56
  11.4 0.1 slice_maximum_fusion.5
  11.5 0.1 fusion.81
  11.9 0.1 slice_maximum_fusion.4
  12.0 0.1 fusion.79
  12.1 0.1 fusion.84
  12.2 0.1 fusion.87
  13.1 0.1 fusion.16
  13.2 0.1 fusion.20
  13.3 0.8 %copy-done.1 = bf16[1,2,4,3,12,1,128]{6,2,5,4,3,1,0:T(4,128)(2,1)S(1)} copy-done((bf16[1,2,4,3,12,1,128]{6,2,5,4,3,1,0:T(4,128)(2,1)S(1)}, bf16[1,2,4,3,12,1,128]{6,2,5,4,3,1,0:T(4,128)(2,1)}, u32[]{:S(2)}) %copy-start.1) | copy-done | bytes 73752
  14.2 0.1 slice_maximum_fusion.3
  14.3 0.1 fusion.71
  15.1 0.1 fusion.46
  15.2 0.1 fusion.47
  15.3 0.1 fusion.49
  15.4 0.1 fusion.50
  15.5 0.1 fusion.77
  15.8 1.3 %collective-permute-start.6 = (bf16[1,2,2,3,12,1,128]{6,4,3,2,5,1,0:T(8,128)(2,1)S(1)}, bf16[1,2,2,3,12,1,128]{6,4,3,2,5,1,0:T(8,128)(2,1)S(1)}, u32[]{:S(2)}, u32[]{:S(2)}) collective-permute-start(bf16[1,2,2,3,12,1,128]{6,4,3,2,5,1,0:T(8,128)(2,1)S(1)} %pad_maximum_fusion.37), channel_id=1, source_target_pairs={{8,0},{16,8},{24,16},{0,24},{9,1},{17,9},{25,17},{1,25},{10,2},{18... | collective-permute-start | bytes 110600 | tf_op jit(solution)/shard_map/ppermute | solution.py:21
  17.2 0.1 collective-permute-start.7
  17.3 0.1 collective-permute-start.5
  17.4 4.8 %collective-permute-start.4 = (bf16[1,2,2,3,12,1,128]{6,4,3,2,5,1,0:T(8,128)(2,1)S(1)}, bf16[1,2,2,3,12,1,128]{6,4,3,2,5,1,0:T(8,128)(2,1)S(1)}, u32[]{:S(2)}, u32[]{:S(2)}) collective-permute-start(bf16[1,2,2,3,12,1,128]{6,4,3,2,5,1,0:T(8,128)(2,1)S(1)} %pad_maximum_fusion.33), channel_id=1, source_target_pairs={{1,0},{2,1},{3,2},{4,3},{5,4},{6,5},{7,6},{0,7},{9,8},{10,9},{11,1... | collective-permute-start | bytes 110600 | tf_op jit(solution)/shard_map/ppermute | solution.py:21
  22.2 0.1 slice_maximum_fusion.2
  22.3 0.1 fusion.69
  22.4 0.1 fusion.74
  22.8 1.2 %collective-permute-done.4 = bf16[1,2,2,3,12,1,128]{6,4,3,2,5,1,0:T(8,128)(2,1)S(1)} collective-permute-done((bf16[1,2,2,3,12,1,128]{6,4,3,2,5,1,0:T(8,128)(2,1)S(1)}, bf16[1,2,2,3,12,1,128]{6,4,3,2,5,1,0:T(8,128)(2,1)S(1)}, u32[]{:S(2)}, u32[]{:S(2)}) %collective-permute-start.4) | collective-permute-done | bytes 36896 | tf_op jit(solution)/shard_map/ppermute | solution.py:21
  24.5 0.1 fusion.24
  24.6 0.1 fusion.28
  24.8 0.1 slice_maximum_fusion.1
  24.9 0.1 fusion.61
  25.7 0.1 fusion.40
  25.8 0.1 fusion.41
  25.9 0.1 fusion.43
  26.0 0.1 fusion.44
  26.2 0.1 fusion.67
  26.4 1.0 %collective-permute-start.10 = (bf16[1,2,2,3,12,1,128]{6,4,3,2,5,1,0:T(8,128)(2,1)S(1)}, bf16[1,2,2,3,12,1,128]{6,4,3,2,5,1,0:T(8,128)(2,1)S(1)}, u32[]{:S(2)}, u32[]{:S(2)}) collective-permute-start(bf16[1,2,2,3,12,1,128]{6,4,3,2,5,1,0:T(8,128)(2,1)S(1)} %pad_maximum_fusion.49), channel_id=1, source_target_pairs={{8,0},{16,8},{24,16},{0,24},{9,1},{17,9},{25,17},{1,25},{10,2},{18... | collective-permute-start | bytes 110600 | tf_op jit(solution)/shard_map/ppermute | solution.py:21
  27.5 0.1 collective-permute-start.11
  27.6 0.1 collective-permute-start.9
  27.7 4.8 %collective-permute-start.8 = (bf16[1,2,2,3,12,1,128]{6,4,3,2,5,1,0:T(8,128)(2,1)S(1)}, bf16[1,2,2,3,12,1,128]{6,4,3,2,5,1,0:T(8,128)(2,1)S(1)}, u32[]{:S(2)}, u32[]{:S(2)}) collective-permute-start(bf16[1,2,2,3,12,1,128]{6,4,3,2,5,1,0:T(8,128)(2,1)S(1)} %pad_maximum_fusion.45), channel_id=1, source_target_pairs={{1,0},{2,1},{3,2},{4,3},{5,4},{6,5},{7,6},{0,7},{9,8},{10,9},{11,1... | collective-permute-start | bytes 110600 | tf_op jit(solution)/shard_map/ppermute | solution.py:21
  32.6 0.1 slice_maximum_fusion
  32.6 0.1 fusion.59
  32.8 0.1 fusion.64
  33.2 1.2 %collective-permute-done.8 = bf16[1,2,2,3,12,1,128]{6,4,3,2,5,1,0:T(8,128)(2,1)S(1)} collective-permute-done((bf16[1,2,2,3,12,1,128]{6,4,3,2,5,1,0:T(8,128)(2,1)S(1)}, bf16[1,2,2,3,12,1,128]{6,4,3,2,5,1,0:T(8,128)(2,1)S(1)}, u32[]{:S(2)}, u32[]{:S(2)}) %collective-permute-start.8) | collective-permute-done | bytes 36896 | tf_op jit(solution)/shard_map/ppermute | solution.py:21
  34.7 0.1 fusion.32
  34.8 0.1 fusion.36
  35.0 0.2 convolution_bitcast_fusion
  35.2 38.5 %psum.7 = f32[1,2,4,12,128]{4,3,2,1,0:T(8,128)S(1)} all-reduce(f32[1,2,4,12,128]{4,3,2,1,0:T(8,128)S(1)} %convolution_bitcast_fusion), channel_id=1, replica_groups=mesh['tm'=4,'space'=8] {'space'}, use_global_device_ids=true, to_apply=%region_0.1 | all-reduce | flops 12288 | bytes 98304 | tf_op jit(solution)/shard_map/psum | solution.py:194
  73.7 0.2 fusion.88
  73.8 0.2 fusion.89
  74.0 0.2 fusion.1
  74.2 0.2 fusion
  74.4 0.6 copy.426
  75.0 0.1 constant_dynamic-slice_fusion
  75.1 0.6 copy.425
  (310 shorter events, 4.2 us)
Async XLA Ops:
  0.6 34.3 %copy-start = (bf16[1,128,2,3,1,128]{5,2,4,3,1,0:T(2,128)(2,1)S(1)}, bf16[1,128,2,3,1,128]{5,2,4,3,1,0:T(2,128)(2,1)}, u32[]{:S(2)}) copy-start(bf16[1,128,2,3,1,128]{5,2,4,3,1,0:T(2,128)(2,1)} %param.6) | copy-start | bytes 589828
  1.7 0.7 copy-start.3
  2.6 10.0 %collective-permute-start.3 = (bf16[1,2,2,3,12,1,128]{6,4,3,2,5,1,0:T(8,128)(2,1)S(1)}, bf16[1,2,2,3,12,1,128]{6,4,3,2,5,1,0:T(8,128)(2,1)S(1)}, u32[]{:S(2)}, u32[]{:S(2)}) collective-permute-start(bf16[1,2,2,3,12,1,128]{6,4,3,2,5,1,0:T(8,128)(2,1)S(1)} %pad_maximum_fusion.27), channel_id=1, source_target_pairs={{0,8},{8,16},{16,24},{24,0},{1,9},{9,17},{17,25},{25,1},{2,10},{10... | collective-permute-start | bytes 110600 | tf_op jit(solution)/shard_map/ppermute | solution.py:20
  3.3 9.3 %collective-permute-start.1 = (bf16[1,2,2,3,12,1,128]{6,4,3,2,5,1,0:T(8,128)(2,1)S(1)}, bf16[1,2,2,3,12,1,128]{6,4,3,2,5,1,0:T(8,128)(2,1)S(1)}, u32[]{:S(2)}, u32[]{:S(2)}) collective-permute-start(bf16[1,2,2,3,12,1,128]{6,4,3,2,5,1,0:T(8,128)(2,1)S(1)} %pad_maximum_fusion.24), channel_id=1, source_target_pairs={{0,1},{1,2},{2,3},{3,4},{4,5},{5,6},{6,7},{7,0},{8,9},{9,10},{10,1... | collective-permute-start | bytes 110600 | tf_op jit(solution)/shard_map/ppermute | solution.py:20
  6.0 6.7 %collective-permute-start = (bf16[1,2,2,3,12,1,128]{6,4,3,2,5,1,0:T(8,128)(2,1)S(1)}, bf16[1,2,2,3,12,1,128]{6,4,3,2,5,1,0:T(8,128)(2,1)S(1)}, u32[]{:S(2)}, u32[]{:S(2)}) collective-permute-start(bf16[1,2,2,3,12,1,128]{6,4,3,2,5,1,0:T(8,128)(2,1)S(1)} %pad_maximum_fusion.21), channel_id=1, source_target_pairs={{1,0},{2,1},{3,2},{4,3},{5,4},{6,5},{7,6},{0,7},{9,8},{10,9},{11,1... | collective-permute-start | bytes 110600 | tf_op jit(solution)/shard_map/ppermute | solution.py:21
  9.1 3.8 %collective-permute-start.2 = (bf16[1,2,2,3,12,1,128]{6,4,3,2,5,1,0:T(8,128)(2,1)S(1)}, bf16[1,2,2,3,12,1,128]{6,4,3,2,5,1,0:T(8,128)(2,1)S(1)}, u32[]{:S(2)}, u32[]{:S(2)}) collective-permute-start(bf16[1,2,2,3,12,1,128]{6,4,3,2,5,1,0:T(8,128)(2,1)S(1)} %pad_maximum_fusion.25), channel_id=1, source_target_pairs={{8,0},{16,8},{24,16},{0,24},{9,1},{17,9},{25,17},{1,25},{10,2},{18... | collective-permute-start | bytes 110600 | tf_op jit(solution)/shard_map/ppermute | solution.py:21
  13.2 0.9 %copy-start.1 = (bf16[1,2,4,3,12,1,128]{6,2,5,4,3,1,0:T(4,128)(2,1)S(1)}, bf16[1,2,4,3,12,1,128]{6,2,5,4,3,1,0:T(4,128)(2,1)}, u32[]{:S(2)}) copy-start(bf16[1,2,4,3,12,1,128]{6,2,5,4,3,1,0:T(4,128)(2,1)} %param.4) | copy-start | bytes 221188
  15.8 6.9 %collective-permute-start.6 = (bf16[1,2,2,3,12,1,128]{6,4,3,2,5,1,0:T(8,128)(2,1)S(1)}, bf16[1,2,2,3,12,1,128]{6,4,3,2,5,1,0:T(8,128)(2,1)S(1)}, u32[]{:S(2)}, u32[]{:S(2)}) collective-permute-start(bf16[1,2,2,3,12,1,128]{6,4,3,2,5,1,0:T(8,128)(2,1)S(1)} %pad_maximum_fusion.37), channel_id=1, source_target_pairs={{8,0},{16,8},{24,16},{0,24},{9,1},{17,9},{25,17},{1,25},{10,2},{18... | collective-permute-start | bytes 110600 | tf_op jit(solution)/shard_map/ppermute | solution.py:21
  17.2 7.1 %collective-permute-start.7 = (bf16[1,2,2,3,12,1,128]{6,4,3,2,5,1,0:T(8,128)(2,1)S(1)}, bf16[1,2,2,3,12,1,128]{6,4,3,2,5,1,0:T(8,128)(2,1)S(1)}, u32[]{:S(2)}, u32[]{:S(2)}) collective-permute-start(bf16[1,2,2,3,12,1,128]{6,4,3,2,5,1,0:T(8,128)(2,1)S(1)} %pad_maximum_fusion.39), channel_id=1, source_target_pairs={{0,8},{8,16},{16,24},{24,0},{1,9},{9,17},{17,25},{25,1},{2,10},{10... | collective-permute-start | bytes 110600 | tf_op jit(solution)/shard_map/ppermute | solution.py:20
  17.3 7.0 %collective-permute-start.5 = (bf16[1,2,2,3,12,1,128]{6,4,3,2,5,1,0:T(8,128)(2,1)S(1)}, bf16[1,2,2,3,12,1,128]{6,4,3,2,5,1,0:T(8,128)(2,1)S(1)}, u32[]{:S(2)}, u32[]{:S(2)}) collective-permute-start(bf16[1,2,2,3,12,1,128]{6,4,3,2,5,1,0:T(8,128)(2,1)S(1)} %pad_maximum_fusion.36), channel_id=1, source_target_pairs={{0,1},{1,2},{2,3},{3,4},{4,5},{5,6},{6,7},{7,0},{8,9},{9,10},{10,1... | collective-permute-start | bytes 110600 | tf_op jit(solution)/shard_map/ppermute | solution.py:20
  17.4 6.6 %collective-permute-start.4 = (bf16[1,2,2,3,12,1,128]{6,4,3,2,5,1,0:T(8,128)(2,1)S(1)}, bf16[1,2,2,3,12,1,128]{6,4,3,2,5,1,0:T(8,128)(2,1)S(1)}, u32[]{:S(2)}, u32[]{:S(2)}) collective-permute-start(bf16[1,2,2,3,12,1,128]{6,4,3,2,5,1,0:T(8,128)(2,1)S(1)} %pad_maximum_fusion.33), channel_id=1, source_target_pairs={{1,0},{2,1},{3,2},{4,3},{5,4},{6,5},{7,6},{0,7},{9,8},{10,9},{11,1... | collective-permute-start | bytes 110600 | tf_op jit(solution)/shard_map/ppermute | solution.py:21
  26.4 6.6 %collective-permute-start.10 = (bf16[1,2,2,3,12,1,128]{6,4,3,2,5,1,0:T(8,128)(2,1)S(1)}, bf16[1,2,2,3,12,1,128]{6,4,3,2,5,1,0:T(8,128)(2,1)S(1)}, u32[]{:S(2)}, u32[]{:S(2)}) collective-permute-start(bf16[1,2,2,3,12,1,128]{6,4,3,2,5,1,0:T(8,128)(2,1)S(1)} %pad_maximum_fusion.49), channel_id=1, source_target_pairs={{8,0},{16,8},{24,16},{0,24},{9,1},{17,9},{25,17},{1,25},{10,2},{18... | collective-permute-start | bytes 110600 | tf_op jit(solution)/shard_map/ppermute | solution.py:21
  27.5 7.0 %collective-permute-start.11 = (bf16[1,2,2,3,12,1,128]{6,4,3,2,5,1,0:T(8,128)(2,1)S(1)}, bf16[1,2,2,3,12,1,128]{6,4,3,2,5,1,0:T(8,128)(2,1)S(1)}, u32[]{:S(2)}, u32[]{:S(2)}) collective-permute-start(bf16[1,2,2,3,12,1,128]{6,4,3,2,5,1,0:T(8,128)(2,1)S(1)} %pad_maximum_fusion.51), channel_id=1, source_target_pairs={{0,8},{8,16},{16,24},{24,0},{1,9},{9,17},{17,25},{25,1},{2,10},{10... | collective-permute-start | bytes 110600 | tf_op jit(solution)/shard_map/ppermute | solution.py:20
  27.6 6.9 %collective-permute-start.9 = (bf16[1,2,2,3,12,1,128]{6,4,3,2,5,1,0:T(8,128)(2,1)S(1)}, bf16[1,2,2,3,12,1,128]{6,4,3,2,5,1,0:T(8,128)(2,1)S(1)}, u32[]{:S(2)}, u32[]{:S(2)}) collective-permute-start(bf16[1,2,2,3,12,1,128]{6,4,3,2,5,1,0:T(8,128)(2,1)S(1)} %pad_maximum_fusion.48), channel_id=1, source_target_pairs={{0,1},{1,2},{2,3},{3,4},{4,5},{5,6},{6,7},{7,0},{8,9},{9,10},{10,1... | collective-permute-start | bytes 110600 | tf_op jit(solution)/shard_map/ppermute | solution.py:20
  27.7 6.6 %collective-permute-start.8 = (bf16[1,2,2,3,12,1,128]{6,4,3,2,5,1,0:T(8,128)(2,1)S(1)}, bf16[1,2,2,3,12,1,128]{6,4,3,2,5,1,0:T(8,128)(2,1)S(1)}, u32[]{:S(2)}, u32[]{:S(2)}) collective-permute-start(bf16[1,2,2,3,12,1,128]{6,4,3,2,5,1,0:T(8,128)(2,1)S(1)} %pad_maximum_fusion.45), channel_id=1, source_target_pairs={{1,0},{2,1},{3,2},{4,3},{5,4},{6,5},{7,6},{0,7},{9,8},{10,9},{11,1... | collective-permute-start | bytes 110600 | tf_op jit(solution)/shard_map/ppermute | solution.py:21
  35.2 38.5 %copy-start.2 = (f32[1,2,16,128]{3,2,1,0:T(8,128)S(1)}, f32[1,2,16,128]{3,2,1,0:T(8,128)}, u32[]{:S(2)}) copy-start(f32[1,2,16,128]{3,2,1,0:T(8,128)} %param.7) | copy-start | bytes 49156
where the time goes:
time: 76 us; the launch traced here: 75.7 us
  blocking collectives  38.5 us (51%)
  starting transfers between devices  19.8 us (26%)
  other arithmetic  7.8 us (10%)
  local copies, waits for them, and re-layouts  3.32 us (4%)
  between operations  3.13 us (4%)
  waiting for transfers between devices  2.41 us (3%)
  matrix products  0.85 us (1%)
    psum x1, blocking collectives, local(): totals = lax.psum(partial_value, 'space')  38.5 us
    ppermute x6, starting transfers between devices, with_halo(): after = lax.ppermute(leading, axis, down)  16.5 us
    ppermute x6, starting transfers between devices, with_halo(): before = lax.ppermute(last, axis, up)  3.3 us
    unnamed x10, local copies, waits for them, and re-layouts  2.81 us
    ppermute x6, waiting for transfers between devices, with_halo(): after = lax.ppermute(leading, axis, down)  2.4 us
    another operation x83, other arithmetic, stored(): return jnp.stack([pair[0], pair[1]], 1).astype(jnp.bfloat16)  2.28 us
  transfers between devices with their start and end apart: 12, of which 2 were waited for; matrix products, arithmetic and copies ran while one was open for 5% of the time, Pallas kernels for 0%

commit v1 on v0

v1 whole, which is shorter than its diff:
```python
import functools

import jax
import jax.numpy as jnp
from jax import lax
from jax.experimental import pallas as pl
from jax.experimental.pallas import tpu as pltpu
from jax.sharding import PartitionSpec as P

LX = 8
HOPPING = 0.125
SWEEPS = 3
MESH = pl.DeviceIdType.MESH
f32 = jnp.float32
bf16 = jnp.bfloat16


def each(lower, upper, body):
    if upper - lower <= 16:
        for index in range(lower, upper):
            body(index)
    else:
        lax.fori_loop(lower, upper, lambda index, carry: (body(index), carry)[1], 0)


def kernel(
    slices, peers, nsrc, modes_dev,
    src_hbm, link_hbm, vec_hbm, elem_hbm,
    proj_ref, cont_ref,
    src_in, link_in, vec_in, elem_in, load_sem,
    wide, link_wide, links, base, field, swap, vec_wide,
    halo_out, halo_in, halo_send, halo_recv,
    elem_all, elem_full, elem_send, elem_recv,
    left_mat, right_mat, sums, part_out, part_in, part_send, part_recv, turned,
):
    rows = 2 * nsrc
    tiles = rows // 8
    lanes = base.shape[-1]
    nmode = peers * modes_dev
    t = lax.axis_index("tm")
    me = lax.axis_index("space")
    t_up, t_down = lax.rem(t + 1, slices), lax.rem(t + slices - 1, slices)
    z_up, z_down = lax.rem(me + 1, peers), lax.rem(me + peers - 1, peers)

    barrier = pltpu.get_barrier_semaphore()

    def greet(off):
        pl.semaphore_signal(
            barrier, inc=1, device_id=(t, lax.rem(me + off, peers)), device_id_type=MESH
        )

    for near in (t_up, t_down):
        pl.semaphore_signal(barrier, inc=1, device_id=(near, me), device_id_type=MESH)
    each(1, peers, greet)

    loads = [
        pltpu.make_async_copy(a, b, load_sem.at[i])
        for i, (a, b) in enumerate(
            ((src_hbm, src_in), (link_hbm, link_in), (elem_hbm, elem_in), (vec_hbm, vec_in))
        )
    ]
    for load in loads:
        load.start()

    loads[1].wait()
    link_wide[...] = link_in[...].astype(f32)
    for mu in range(4):
        for i in range(3):
            for j in range(3):
                for part in range(2):
                    row = ((mu * 3 + i) * 3 + j) * 2 + part
                    links[mu, part, i, j] = jnp.broadcast_to(
                        link_wide[row : row + 1, :], (8, lanes)
                    )
    loads[0].wait()
    wide[...] = src_in[...].astype(f32)
    for pc in range(6):
        for spin in range(4):
            piece = wide[pl.ds(pc * 4 * nsrc + spin, nsrc, stride=4), :]
            base[pc, spin * nsrc : (spin + 1) * nsrc, :] = piece
            field[pc, spin * nsrc : (spin + 1) * nsrc, :] = piece
            if spin == 2:
                field[pc, 4 * nsrc : 5 * nsrc, :] = piece

    row_at = lax.broadcasted_iota(jnp.int32, (tiles, 8, lanes), 0) * 8
    row_at = row_at + lax.broadcasted_iota(jnp.int32, (tiles, 8, lanes), 1)
    spin_sign = jnp.where(row_at < nsrc, 1.0, -1.0).astype(f32)[None]
    column = lax.broadcasted_iota(jnp.int32, (1, 1, 8, lanes), 3) % LX
    ahead_sign = jnp.where(t == slices - 1, -1.0, 1.0).astype(f32)
    behind_sign = jnp.where(t == 0, -1.0, 1.0).astype(f32)

    def tiled(value):
        return value.reshape(3, tiles, 8, lanes)

    def apply(mu, pair, dagger):
        re, im = pair
        out_re = out_im = None
        for j in range(3):
            if dagger:
                g_re, g_im = links[mu, 0, j], links[mu, 1, j]
            else:
                g_re, g_im = links[mu, 0, :, j], links[mu, 1, :, j]
            g_re, g_im = g_re[:, None], g_im[:, None]
            v_re, v_im = re[j][None], im[j][None]
            if dagger:
                add_re, add_im = g_re * v_re + g_im * v_im, g_re * v_im - g_im * v_re
            else:
                add_re, add_im = g_re * v_re - g_im * v_im, g_re * v_im + g_im * v_re
            out_re = add_re if out_re is None else out_re + add_re
            out_im = add_im if out_im is None else out_im + add_im
        return out_re, out_im

    def shift(pair, direction, ahead):
        out = []
        for v in pair:
            flat = v.reshape(3 * rows, lanes)
            if direction == 1:
                got = pltpu.roll(flat, lanes - LX if ahead else LX, 1)
                out.append(tiled(got))
            else:
                near = tiled(pltpu.roll(flat, lanes - 1 if ahead else 1, 1))
                wrap = tiled(pltpu.roll(flat, LX - 1 if ahead else lanes - LX + 1, 1))
                out.append(jnp.where(column == (LX - 1 if ahead else 0), wrap, near))
        return tuple(out)

    def packed(pair):
        return jnp.concatenate([v.reshape(3 * rows, lanes) for v in pair], 0).astype(bf16)

    def unpacked(value):
        value = value.astype(f32)
        return tiled(value[: 3 * rows]), tiled(value[3 * rows :])

    def halo(sweep, way):
        target = ((t_down, me), (t_up, me), (t, z_down), (t, z_up))[way]
        return pltpu.make_async_remote_copy(
            src_ref=halo_out.at[sweep, way],
            dst_ref=halo_in.at[sweep, way],
            send_sem=halo_send.at[sweep, way],
            recv_sem=halo_recv.at[sweep, way],
            device_id=target,
            device_id_type=MESH,
        )

    def elem_copy(to, slot):
        return pltpu.make_async_remote_copy(
            src_ref=elem_all.at[me],
            dst_ref=elem_all.at[slot],
            send_sem=elem_send.at[to],
            recv_sem=elem_recv.at[slot],
            device_id=(t, to),
            device_id_type=MESH,
        )

    def part_copy(to, slot):
        return pltpu.make_async_remote_copy(
            src_ref=part_out.at[to],
            dst_ref=part_in.at[slot],
            send_sem=part_send.at[to],
            recv_sem=part_recv.at[slot],
            device_id=(t, to),
            device_id_type=MESH,
        )

    for sweep in range(SWEEPS):
        up = [tiled(field[3 * i : 3 * i + 3, 0:rows, :]) for i in range(2)]
        low = [tiled(field[3 * i : 3 * i + 3, rows : 2 * rows, :]) for i in range(2)]
        turn = (spin_sign * low[1], -(spin_sign * low[0]))
        sent = [halo(sweep, way) for way in range(4)]
        halo_out[sweep, 2] = packed((up[0] - turn[0], up[1] - turn[1]))
        if sweep == 0:
            pl.semaphore_wait(barrier, peers + 1)
        sent[2].start()
        halo_out[sweep, 3] = packed(apply(2, (up[0] + turn[0], up[1] + turn[1]), True))
        sent[3].start()
        halo_out[sweep, 0] = packed((up[0] - low[0], up[1] - low[1]))
        sent[0].start()
        halo_out[sweep, 1] = packed(apply(3, (up[0] + low[0], up[1] + low[1]), True))
        sent[1].start()

        if sweep == 0:
            loads[2].wait()
            elem_all[me] = elem_in[...].astype(elem_all.dtype)
            each(1, peers, lambda off: elem_copy(lax.rem(me + off, peers), me).start())

        swapped = [
            tiled(field[3 * i : 3 * i + 3, rows + nsrc : 2 * rows + nsrc, :]) for i in range(2)
        ]
        turned_x = (swapped[1], -swapped[0])
        turned_y = (-(spin_sign * swapped[0]), -(spin_sign * swapped[1]))
        ahead = {}
        behind = {}
        for mu, moved in ((0, turned_x), (1, turned_y)):
            ahead[mu] = apply(
                mu, shift((up[0] - moved[0], up[1] - moved[1]), mu, True), False
            )
            behind[mu] = shift(
                apply(mu, (up[0] + moved[0], up[1] + moved[1]), True), mu, False
            )
        upper = [ahead[0][i] + behind[0][i] + ahead[1][i] + behind[1][i] for i in range(2)]
        dx = [behind[0][i] - ahead[0][i] for i in range(2)]
        dy = [behind[1][i] - ahead[1][i] for i in range(2)]
        cross = (-dx[1] - spin_sign * dy[0], dx[0] - spin_sign * dy[1])
        for i in range(2):
            flat = cross[i].reshape(3, rows, lanes)
            swap[3 * i : 3 * i + 3, 0:rows, :] = flat
            swap[3 * i : 3 * i + 3, rows : rows + nsrc, :] = flat[:, :nsrc]
        lower = [tiled(swap[3 * i : 3 * i + 3, nsrc : nsrc + rows, :]) for i in range(2)]

        if sweep == 0:
            loads[3].wait()
            vec_wide[...] = vec_in[...].astype(f32)
            for j in range(6):
                left_mat[0:nmode, j * lanes : (j + 1) * lanes] = vec_wide[
                    pl.ds(j, nmode, stride=6), :
                ].astype(bf16)
        if sweep == 1:
            each(
                1, peers,
                lambda off: elem_copy(lax.rem(me + off, peers), lax.rem(me + off, peers)).wait_recv(),
            )
            for p in range(peers):
                for part in range(2):
                    elem_full[part, p * modes_dev : (p + 1) * modes_dev, :] = elem_all[
                        p, part
                    ].astype(f32)
            e_re, e_im = elem_full[0].astype(bf16), elem_full[1].astype(bf16)
            blocks = jnp.concatenate(
                [
                    jnp.concatenate([e_re, e_im], 1),
                    jnp.concatenate([-e_im, e_re], 1),
                ],
                0,
            )
            for c in range(3):
                both = jnp.concatenate(
                    [
                        left_mat[0:nmode, (2 * c + part) * lanes : (2 * c + part + 1) * lanes]
                        for part in range(2)
                    ],
                    0,
                )
                mixed = jnp.dot(blocks, both, preferred_element_type=f32).astype(bf16)
                for part in range(2):
                    left_mat[
                        nmode : 2 * nmode, (2 * c + part) * lanes : (2 * c + part + 1) * lanes
                    ] = mixed[part * nmode : (part + 1) * nmode]

        sent[0].wait_recv()
        f_t = apply(3, unpacked(halo_in[sweep, 0]), False)
        sent[1].wait_recv()
        b_t = unpacked(halo_in[sweep, 1])
        f_t = [ahead_sign * v for v in f_t]
        b_t = [behind_sign * v for v in b_t]
        upper = [upper[i] + f_t[i] + b_t[i] for i in range(2)]
        lower = [lower[i] + b_t[i] - f_t[i] for i in range(2)]
        sent[2].wait_recv()
        f_z = apply(2, unpacked(halo_in[sweep, 2]), False)
        sent[3].wait_recv()
        b_z = unpacked(halo_in[sweep, 3])
        dz = [b_z[i] - f_z[i] for i in range(2)]
        upper = [upper[i] + f_z[i] + b_z[i] for i in range(2)]
        lower = [lower[0] - spin_sign * dz[1], lower[1] + spin_sign * dz[0]]
        for i in range(2):
            at = slice(3 * i, 3 * i + 3)
            new_up = base[at, 0:rows, :] + HOPPING * upper[i].reshape(3, rows, lanes)
            new_low = base[at, rows : 2 * rows, :] + HOPPING * lower[i].reshape(3, rows, lanes)
            new_up = new_up.astype(bf16).astype(f32)
            new_low = new_low.astype(bf16).astype(f32)
            field[at, 0:rows, :] = new_up
            field[at, rows : 2 * rows, :] = new_low
            if sweep < SWEEPS - 1:
                field[at, 2 * rows : 2 * rows + nsrc, :] = new_low[:, :nsrc]

    for pc in range(6):
        for spin in range(4):
            wide[pl.ds(pc * 4 * nsrc + spin, nsrc, stride=4), :] = field[
                pc, spin * nsrc : (spin + 1) * nsrc, :
            ]
    count = 4 * nsrc
    for c in range(3):
        re = wide[c * count : (c + 1) * count, :]
        im = wide[(3 + c) * count : (4 + c) * count, :]
        at = 2 * c * lanes
        right_mat[:, at : at + lanes] = jnp.concatenate([re, im], 0).astype(bf16)
        right_mat[:, at + lanes : at + 2 * lanes] = jnp.concatenate([im, -re], 0).astype(bf16)
    sums[:, 0 : 2 * count] = lax.dot_general(
        left_mat[...], right_mat[...], (((1,), (1,)), ((), ())), preferred_element_type=f32
    )
    for p in range(peers):
        for o in range(2):
            at = o * nmode + p * modes_dev
            part_out[p, o] = sums[at : at + modes_dev, :].astype(part_out.dtype)
    each(1, peers, lambda off: part_copy(lax.rem(me + off, peers), me).start())

    turned[...] = jnp.zeros_like(turned)
    for o in range(2):
        turned[o * modes_dev : (o + 1) * modes_dev, :] = part_out[me, o].astype(f32)

    def gather(off):
        p = lax.rem(me + off, peers)
        part_copy(p, p).wait_recv()
        for o in range(2):
            turned[o * modes_dev : (o + 1) * modes_dev, :] += part_in[p, o].astype(f32)

    each(1, peers, gather)
    flipped = turned[...].T
    proj_ref[...] = flipped[0 : 2 * count, 0:modes_dev]
    cont_ref[...] = flipped[0 : 2 * count, modes_dev : 2 * modes_dev]

    for sweep in range(SWEEPS):
        for way in range(4):
            halo(sweep, way).wait_send()

    def settle(off):
        p = lax.rem(me + off, peers)
        elem_copy(p, me).wait_send()
        part_copy(p, me).wait_send()

    each(1, peers, settle)


def local(sources, gauge_links, eigenvectors, elementals):
    slices, peers = lax.axis_size("tm"), lax.axis_size("space")
    _, _, _, _, nsrc, _, lanes = sources.shape
    nmode = eigenvectors.shape[1]
    modes_dev = elementals.shape[2]
    src = sources.transpose(0, 1, 3, 4, 5, 2, 6).reshape(24 * nsrc, lanes)
    link = gauge_links.transpose(0, 1, 3, 4, 5, 2, 6).reshape(72, lanes)
    vec = eigenvectors.transpose(0, 1, 3, 4, 2, 5).reshape(6 * nmode, lanes)
    elem = elementals.reshape(2, modes_dev, nmode)
    rows = 2 * nsrc
    kind = bf16 if modes_dev % 16 == 0 else f32
    outs = jax.ShapeDtypeStruct((8 * nsrc, modes_dev), f32)
    dma = pltpu.SemaphoreType.DMA
    proj, cont = pl.pallas_call(
        functools.partial(kernel, slices, peers, nsrc, modes_dev),
        out_shape=(outs, outs),
        in_specs=[pl.BlockSpec(memory_space=pl.ANY)] * 4,
        out_specs=[pl.BlockSpec(memory_space=pltpu.VMEM)] * 2,
        scratch_shapes=[
            pltpu.VMEM(src.shape, bf16),
            pltpu.VMEM(link.shape, bf16),
            pltpu.VMEM(vec.shape, bf16),
            pltpu.VMEM(elem.shape, f32),
            dma((4,)),
            pltpu.VMEM(src.shape, f32),
            pltpu.VMEM(link.shape, f32),
            pltpu.VMEM((4, 2, 3, 3, 8, lanes), f32),
            pltpu.VMEM((6, 2 * rows, lanes), f32),
            pltpu.VMEM((6, 2 * rows + 16, lanes), f32),
            pltpu.VMEM((6, rows + 16, lanes), f32),
            pltpu.VMEM(vec.shape, f32),
            pltpu.VMEM((SWEEPS, 4, 6 * rows, lanes), bf16),
            pltpu.VMEM((SWEEPS, 4, 6 * rows, lanes), bf16),
            dma((SWEEPS, 4)),
            dma((SWEEPS, 4)),
            pltpu.VMEM((peers, 2, modes_dev, nmode), kind),
            pltpu.VMEM((2, nmode, nmode), f32),
            dma((peers,)),
            dma((peers,)),
            pltpu.VMEM((2 * nmode, 6 * lanes), bf16),
            pltpu.VMEM((8 * nsrc, 6 * lanes), bf16),
            pltpu.VMEM((2 * nmode, 128), f32),
            pltpu.VMEM((peers, 2, modes_dev, 128), kind),
            pltpu.VMEM((peers, 2, modes_dev, 128), kind),
            dma((peers,)),
            dma((peers,)),
            pltpu.VMEM((128, 128), f32),
        ],
        compiler_params=pltpu.CompilerParams(
            collective_id=0, has_side_effects=True, vmem_limit_bytes=32 * 1024 * 1024
        ),
        cost_estimate=pl.CostEstimate(
            flops=200_000_000, bytes_accessed=1_000_000, transcendentals=0
        ),
    )(src, link, vec, elem)

    def placed(out):
        return out.reshape(1, 2, nsrc, 4, modes_dev).transpose(0, 1, 3, 2, 4)

    return placed(proj), placed(cont)


def solution(mesh):
    placed = (
        P("tm", None, None, None, None, "space", None),
        P(None, "tm", None, None, None, "space", None),
        P("tm", None, None, None, "space", None),
        P("tm", None, "space", None),
    )
    return jax.shard_map(
        local,
        mesh=mesh,
        in_specs=placed,
        out_specs=(P("tm", None, None, None, "space"), P("tm", None, None, None, "space")),
        check_vma=False,
    )
```

time: 76 us -> 29.6 us (0.39)
  blocking collectives: 38.5 us -> 0 us
  Pallas kernels: 0 us -> 24.1 us
  starting transfers between devices: 19.8 us -> 0 us
  other arithmetic: 7.8 us -> 0 us
  between operations: 3.13 us -> 0.65 us
  waiting for transfers between devices: 2.41 us -> 0 us
  local copies, waits for them, and re-layouts: 3.32 us -> 4.48 us
  matrix products: 0.85 us -> 0 us
    psum x1 -> x0, blocking collectives: 38.5 us -> none  [local(): totals = lax.psum(partial_value, 'space')]
    pallas_call x0 -> x1, Pallas kernels: none -> 24.1 us  [local(): pl.pallas_call(functools.partial(kernel, slices, peers, nsrc, modes_dev),...]
    ppermute x12 -> x0, starting transfers between devices: 19.8 us -> none  [the longest x6 16.5 us: with_halo(): after = lax.ppermute(leading, axis, down)]
    another operation x205 -> x0, other arithmetic: 4.33 us -> none  [the longest x83 2.28 us: stored(): return jnp.stack([pair[0], pair[1]], 1).astype(jnp.bfloat16)]
    ppermute x12 -> x0, waiting for transfers between devices: 2.41 us -> none  [the longest x6 2.4 us: with_halo(): after = lax.ppermute(leading, axis, down)]
    convert_element_type x23 -> x0, other arithmetic: 2.24 us -> none  [the longest x21 1.26 us: split_parts(): widened = values.astype(jnp.float32)]
    unnamed x10, local copies, waits for them, and re-layouts: 2.81 us -> 4.48 us
    dot_general x5 -> x0, matrix products: 0.85 us -> none  [the longest x4 0.63 us: product(): return jnp.einsum('tkl,tasl->task', left, right, precision=highest)]
  transfers between devices with their start and end apart: 12 -> 0, of which waited for: 2 -> 0; matrix products, arithmetic and copies ran while one was open for 5% -> 0% of each run, Pallas kernels for 0% -> 0%
where the time goes in v1:
time: 29.6 us; the launch traced here: 29.3 us
  Pallas kernels  24.1 us (81%)
  local copies, waits for them, and re-layouts  4.48 us (15%)
  between operations  0.65 us (2%)
    pallas_call x1, Pallas kernels, local(): pl.pallas_call(functools.partial(kernel, slices, peers, nsrc, modes_dev),...  24.1 us
    unnamed x10, local copies, waits for them, and re-layouts  4.48 us

profile of v1, /device:TPU:0, one launch (start us, length us, event | category | flops | bytes accessed | tf_op | source)
XLA Modules:
  0.0 29.3 jit_solution(6303707227618897734)
XLA Ops:
  0.6 0.0 copy-start
  0.6 0.9 %copy-done = bf16[1,128,2,3,1,128]{5,2,4,3,1,0:T(2,128)(2,1)S(1)} copy-done((bf16[1,128,2,3,1,128]{5,2,4,3,1,0:T(2,128)(2,1)S(1)}, bf16[1,128,2,3,1,128]{5,2,4,3,1,0:T(2,128)(2,1)}, u32[]{:S(2)}) %copy-start) | copy-done | bytes 196632
  1.6 0.0 copy-start.1
  1.6 0.9 %copy-done.1 = bf16[1,2,4,3,12,1,128]{6,2,5,4,3,1,0:T(4,128)(2,1)S(1)} copy-done((bf16[1,2,4,3,12,1,128]{6,2,5,4,3,1,0:T(4,128)(2,1)S(1)}, bf16[1,2,4,3,12,1,128]{6,2,5,4,3,1,0:T(4,128)(2,1)}, u32[]{:S(2)}) %copy-start.1) | copy-done | bytes 73752
  2.4 0.0 copy-start.2
  2.4 0.7 %copy-done.2 = bf16[4,1,2,3,3,1,128]{6,2,5,4,3,1,0:T(2,128)(2,1)S(1)} copy-done((bf16[4,1,2,3,3,1,128]{6,2,5,4,3,1,0:T(2,128)(2,1)S(1)}, bf16[4,1,2,3,3,1,128]{6,2,5,4,3,1,0:T(2,128)(2,1)}, u32[]{:S(2)}) %copy-start.2) | copy-done | bytes 18456
  3.2 0.0 copy-start.3
  3.2 0.7 %copy-done.3 = f32[1,2,16,128]{3,2,1,0:T(8,128)S(1)} copy-done((f32[1,2,16,128]{3,2,1,0:T(8,128)S(1)}, f32[1,2,16,128]{3,2,1,0:T(8,128)}, u32[]{:S(2)}) %copy-start.3) | copy-done | bytes 16408
  3.9 24.1 %shard_map.59 = (f32[96,16]{1,0:T(8,128)S(1)}, f32[96,16]{1,0:T(8,128)S(1)}) custom-call(bf16[288,128]{1,0:T(8,128)(2,1)S(1)} %bitcast.19, bf16[72,128]{1,0:T(8,128)(2,1)S(1)} %bitcast.20, bf16[768,128]{1,0:T(8,128)(2,1)S(1)} %bitcast.18, f32[2,16,128]{2,1,0:T(8,128)S(1)} %bitcast.21), custom_call_target="tpu_custom_call" | custom-call | flops 200000000 | bytes 1000000 | tf_op jit(solution)/shard_map/pallas_call | solution.py:335
  28.0 0.6 %copy.8 = f32[1,2,4,12,16]{4,2,3,1,0:T(4,128)} copy(f32[1,2,4,12,16]{4,2,3,1,0:T(4,128)S(1)} %bitcast.17) | data formatting | bytes 12288
  28.6 0.6 %copy.9 = f32[1,2,4,12,16]{4,2,3,1,0:T(4,128)} copy(f32[1,2,4,12,16]{4,2,3,1,0:T(4,128)S(1)} %bitcast.16) | data formatting | bytes 12288
Async XLA Ops:
  0.6 0.9 %copy-start = (bf16[1,128,2,3,1,128]{5,2,4,3,1,0:T(2,128)(2,1)S(1)}, bf16[1,128,2,3,1,128]{5,2,4,3,1,0:T(2,128)(2,1)}, u32[]{:S(2)}) copy-start(bf16[1,128,2,3,1,128]{5,2,4,3,1,0:T(2,128)(2,1)} %param.6) | copy-start | bytes 589828
  1.6 0.9 %copy-start.1 = (bf16[1,2,4,3,12,1,128]{6,2,5,4,3,1,0:T(4,128)(2,1)S(1)}, bf16[1,2,4,3,12,1,128]{6,2,5,4,3,1,0:T(4,128)(2,1)}, u32[]{:S(2)}) copy-start(bf16[1,2,4,3,12,1,128]{6,2,5,4,3,1,0:T(4,128)(2,1)} %param.4) | copy-start | bytes 221188
  2.4 0.7 %copy-start.2 = (bf16[4,1,2,3,3,1,128]{6,2,5,4,3,1,0:T(2,128)(2,1)S(1)}, bf16[4,1,2,3,3,1,128]{6,2,5,4,3,1,0:T(2,128)(2,1)}, u32[]{:S(2)}) copy-start(bf16[4,1,2,3,3,1,128]{6,2,5,4,3,1,0:T(2,128)(2,1)} %param.5) | copy-start | bytes 55300
  3.2 0.7 %copy-start.3 = (f32[1,2,16,128]{3,2,1,0:T(8,128)S(1)}, f32[1,2,16,128]{3,2,1,0:T(8,128)}, u32[]{:S(2)}) copy-start(f32[1,2,16,128]{3,2,1,0:T(8,128)} %param.7) | copy-start | bytes 49156

commit v2 on v1

v2 whole, which is shorter than its diff:
```python
import functools

import jax
import jax.numpy as jnp
from jax import lax
from jax.experimental import pallas as pl
from jax.experimental.pallas import tpu as pltpu
from jax.sharding import PartitionSpec as P

LX = 8
HOPPING = 0.125
SWEEPS = 3
GROUP = 4
MESH = pl.DeviceIdType.MESH
f32 = jnp.float32
bf16 = jnp.bfloat16


def each(lower, upper, body):
    if upper - lower <= 16:
        for index in range(lower, upper):
            body(index)
    else:
        lax.fori_loop(lower, upper, lambda index, carry: (body(index), carry)[1], 0)


def kernel(
    slices, peers, nsrc, modes_dev,
    src_hbm, link_hbm, vec_hbm, elem_hbm,
    proj_ref, cont_ref,
    src_in, link_in, vec_in, elem_in, load_sem,
    wide, link_wide, links, base, field, hops, vec_wide,
    halo_out, halo_in, halo_send, halo_recv,
    elem_all, elem_full, elem_send, elem_recv,
    left_mat, right_mat, sums, part_out, part_in, part_send, part_recv, turned,
):
    groups = nsrc // GROUP
    half = 2 * GROUP
    lanes = base.shape[-1]
    nmode = peers * modes_dev
    t = lax.axis_index("tm")
    me = lax.axis_index("space")
    t_up, t_down = lax.rem(t + 1, slices), lax.rem(t + slices - 1, slices)
    z_up, z_down = lax.rem(me + 1, peers), lax.rem(me + peers - 1, peers)

    barrier = pltpu.get_barrier_semaphore()

    def greet(off):
        pl.semaphore_signal(
            barrier, inc=1, device_id=(t, lax.rem(me + off, peers)), device_id_type=MESH
        )

    for near in (t_up, t_down):
        pl.semaphore_signal(barrier, inc=1, device_id=(near, me), device_id_type=MESH)
    each(1, peers, greet)

    loads = [
        pltpu.make_async_copy(a, b, load_sem.at[i])
        for i, (a, b) in enumerate(
            ((src_hbm, src_in), (link_hbm, link_in), (elem_hbm, elem_in), (vec_hbm, vec_in))
        )
    ]
    for load in loads:
        load.start()

    row_at = lax.broadcasted_iota(jnp.int32, (1, half, lanes), 1)
    spin_sign = jnp.where(row_at < GROUP, 1.0, -1.0).astype(f32)
    column = lax.broadcasted_iota(jnp.int32, (1, half, lanes), 2) % LX
    ahead_sign = jnp.where(t == slices - 1, -1.0, 1.0).astype(f32)
    behind_sign = jnp.where(t == 0, -1.0, 1.0).astype(f32)

    def apply(mu, pair, dagger):
        re, im = pair
        out_re = out_im = None
        for j in range(3):
            if dagger:
                g_re, g_im = links[mu, 0, j], links[mu, 1, j]
            else:
                g_re, g_im = links[mu, 0, :, j], links[mu, 1, :, j]
            v_re, v_im = re[j][None], im[j][None]
            if dagger:
                add_re, add_im = g_re * v_re + g_im * v_im, g_re * v_im - g_im * v_re
            else:
                add_re, add_im = g_re * v_re - g_im * v_im, g_re * v_im + g_im * v_re
            out_re = add_re if out_re is None else out_re + add_re
            out_im = add_im if out_im is None else out_im + add_im
        return out_re, out_im

    def shift(pair, direction, ahead):
        out = []
        for v in pair:
            if direction == 1:
                out.append(pltpu.roll(v, lanes - LX if ahead else LX, 2))
            else:
                near = pltpu.roll(v, lanes - 1 if ahead else 1, 2)
                wrap = pltpu.roll(v, LX - 1 if ahead else lanes - LX + 1, 2)
                out.append(jnp.where(column == (LX - 1 if ahead else 0), wrap, near))
        return tuple(out)

    def packed(pair):
        return jnp.concatenate([v.reshape(3 * half, lanes) for v in pair], 0).astype(bf16)

    def unpacked(value):
        value = value.astype(f32).reshape(6, half, lanes)
        return value[:3], value[3:]

    def halo(sweep, g, way):
        at = (sweep * groups + g) * 4 + way
        target = ((t_down, me), (t_up, me), (t, z_down), (t, z_up))[way]
        return pltpu.make_async_remote_copy(
            src_ref=halo_out.at[at],
            dst_ref=halo_in.at[at],
            send_sem=halo_send.at[at],
            recv_sem=halo_recv.at[at],
            device_id=target,
            device_id_type=MESH,
        )

    def send(sweep, g, way, pair):
        halo_out[(sweep * groups + g) * 4 + way] = packed(pair)
        halo(sweep, g, way).start()

    def receive(sweep, g, way):
        halo(sweep, g, way).wait_recv()
        return unpacked(halo_in[(sweep * groups + g) * 4 + way])

    def elem_copy(to, slot):
        return pltpu.make_async_remote_copy(
            src_ref=elem_all.at[me],
            dst_ref=elem_all.at[slot],
            send_sem=elem_send.at[to],
            recv_sem=elem_recv.at[slot],
            device_id=(t, to),
            device_id_type=MESH,
        )

    def part_copy(to, slot):
        return pltpu.make_async_remote_copy(
            src_ref=part_out.at[to],
            dst_ref=part_in.at[slot],
            send_sem=part_send.at[to],
            recv_sem=part_recv.at[slot],
            device_id=(t, to),
            device_id_type=MESH,
        )

    def parts_of(g):
        up = [field[g, 3 * i : 3 * i + 3, 0:half, :] for i in range(2)]
        low = [field[g, 3 * i : 3 * i + 3, half : 2 * half, :] for i in range(2)]
        return up, low

    def turn_z(low):
        return spin_sign * low[1], -(spin_sign * low[0])

    def send_minus(sweep, g):
        up, low = parts_of(g)
        turn = turn_z(low)
        send(sweep, g, 2, (up[0] - turn[0], up[1] - turn[1]))
        send(sweep, g, 0, (up[0] - low[0], up[1] - low[1]))

    def send_plus(sweep, g):
        up, low = parts_of(g)
        turn = turn_z(low)
        send(sweep, g, 3, apply(2, (up[0] + turn[0], up[1] + turn[1]), True))
        send(sweep, g, 1, apply(3, (up[0] + low[0], up[1] + low[1]), True))

    def plane(g):
        up, low = parts_of(g)
        swapped = [pltpu.roll(v, GROUP, 1) for v in low]
        turned_x = (swapped[1], -swapped[0])
        turned_y = (-(spin_sign * swapped[0]), -(spin_sign * swapped[1]))
        ahead = {}
        behind = {}
        for mu, moved in ((0, turned_x), (1, turned_y)):
            ahead[mu] = apply(
                mu, shift((up[0] - moved[0], up[1] - moved[1]), mu, True), False
            )
            behind[mu] = shift(
                apply(mu, (up[0] + moved[0], up[1] + moved[1]), True), mu, False
            )
        dx = [behind[0][i] - ahead[0][i] for i in range(2)]
        dy = [behind[1][i] - ahead[1][i] for i in range(2)]
        cross = (-dx[1] - spin_sign * dy[0], dx[0] - spin_sign * dy[1])
        for i in range(2):
            hops[g, i] = ahead[0][i] + behind[0][i] + ahead[1][i] + behind[1][i]
            hops[g, 2 + i] = pltpu.roll(cross[i], GROUP, 1)

    def finish(sweep, g):
        f_t = apply(3, receive(sweep, g, 0), False)
        b_t = receive(sweep, g, 1)
        f_t = [ahead_sign * v for v in f_t]
        b_t = [behind_sign * v for v in b_t]
        f_z = apply(2, receive(sweep, g, 2), False)
        b_z = receive(sweep, g, 3)
        dz = [b_z[i] - f_z[i] for i in range(2)]
        upper = [hops[g, i] + f_t[i] + b_t[i] + f_z[i] + b_z[i] for i in range(2)]
        lower = [hops[g, 2 + i] + b_t[i] - f_t[i] for i in range(2)]
        lower = [lower[0] - spin_sign * dz[1], lower[1] + spin_sign * dz[0]]
        for i in range(2):
            at = slice(3 * i, 3 * i + 3)
            new_up = base[g, at, 0:half, :] + HOPPING * upper[i]
            new_low = base[g, at, half : 2 * half, :] + HOPPING * lower[i]
            field[g, at, 0:half, :] = new_up.astype(bf16).astype(f32)
            field[g, at, half : 2 * half, :] = new_low.astype(bf16).astype(f32)

    loads[0].wait()
    wide[...] = src_in[...].astype(f32)
    for g in range(groups):
        for pc in range(6):
            for spin in range(4):
                piece = wide[pl.ds((pc * nsrc + g * GROUP) * 4 + spin, GROUP, stride=4), :]
                base[g, pc, spin * GROUP : (spin + 1) * GROUP, :] = piece
                field[g, pc, spin * GROUP : (spin + 1) * GROUP, :] = piece
    pl.semaphore_wait(barrier, peers + 1)
    for g in range(groups):
        send_minus(0, g)

    loads[1].wait()
    link_wide[...] = link_in[...].astype(f32)
    for mu in (2, 3, 0, 1):
        for i in range(3):
            for j in range(3):
                for part in range(2):
                    row = ((mu * 3 + i) * 3 + j) * 2 + part
                    links[mu, part, i, j] = jnp.broadcast_to(
                        link_wide[row : row + 1, :], (half, lanes)
                    )
    for g in range(groups):
        send_plus(0, g)

    loads[2].wait()
    elem_all[me] = elem_in[...].astype(elem_all.dtype)
    each(1, peers, lambda off: elem_copy(lax.rem(me + off, peers), me).start())
    for g in range(groups):
        plane(g)

    loads[3].wait()
    vec_wide[...] = vec_in[...].astype(f32)
    for j in range(6):
        left_mat[0:nmode, j * lanes : (j + 1) * lanes] = vec_wide[
            pl.ds(j, nmode, stride=6), :
        ].astype(bf16)

    for sweep in range(1, SWEEPS):
        for g in range(groups):
            finish(sweep - 1, g)
            send_minus(sweep, g)
            send_plus(sweep, g)
        for g in range(groups):
            plane(g)
        if sweep == 1:
            def arrive(off):
                p = lax.rem(me + off, peers)
                elem_copy(p, p).wait_recv()

            each(1, peers, arrive)
            for p in range(peers):
                for part in range(2):
                    elem_full[part, p * modes_dev : (p + 1) * modes_dev, :] = elem_all[
                        p, part
                    ].astype(f32)
            e_re, e_im = elem_full[0].astype(bf16), elem_full[1].astype(bf16)
            blocks = jnp.concatenate(
                [
                    jnp.concatenate([e_re, e_im], 1),
                    jnp.concatenate([-e_im, e_re], 1),
                ],
                0,
            )
            for c in range(3):
                both = jnp.concatenate(
                    [
                        left_mat[0:nmode, (2 * c + part) * lanes : (2 * c + part + 1) * lanes]
                        for part in range(2)
                    ],
                    0,
                )
                mixed = jnp.dot(blocks, both, preferred_element_type=f32).astype(bf16)
                for part in range(2):
                    left_mat[
                        nmode : 2 * nmode, (2 * c + part) * lanes : (2 * c + part + 1) * lanes
                    ] = mixed[part * nmode : (part + 1) * nmode]

    for g in range(groups):
        finish(SWEEPS - 1, g)
        for pc in range(6):
            for spin in range(4):
                wide[pl.ds((pc * nsrc + g * GROUP) * 4 + spin, GROUP, stride=4), :] = field[
                    g, pc, spin * GROUP : (spin + 1) * GROUP, :
                ]
    count = 4 * nsrc
    for c in range(3):
        re = wide[c * count : (c + 1) * count, :]
        im = wide[(3 + c) * count : (4 + c) * count, :]
        at = 2 * c * lanes
        right_mat[:, at : at + lanes] = jnp.concatenate([re, im], 0).astype(bf16)
        right_mat[:, at + lanes : at + 2 * lanes] = jnp.concatenate([im, -re], 0).astype(bf16)
    sums[:, 0 : 2 * count] = lax.dot_general(
        left_mat[...], right_mat[...], (((1,), (1,)), ((), ())), preferred_element_type=f32
    )
    for p in range(peers):
        for o in range(2):
            at = o * nmode + p * modes_dev
            part_out[p, o] = sums[at : at + modes_dev, :].astype(part_out.dtype)
    each(1, peers, lambda off: part_copy(lax.rem(me + off, peers), me).start())

    turned[...] = jnp.zeros_like(turned)
    for o in range(2):
        turned[o * modes_dev : (o + 1) * modes_dev, :] = part_out[me, o].astype(f32)

    def settle(off):
        p = lax.rem(me + off, peers)
        elem_copy(p, me).wait_send()
        part_copy(p, me).wait_send()

    for sweep in range(SWEEPS):
        for g in range(groups):
            for way in range(4):
                halo(sweep, g, way).wait_send()
    each(1, peers, settle)

    def gather(off):
        p = lax.rem(me + off, peers)
        part_copy(p, p).wait_recv()
        for o in range(2):
            turned[o * modes_dev : (o + 1) * modes_dev, :] += part_in[p, o].astype(f32)

    each(1, peers, gather)
    flipped = turned[...].T
    proj_ref[...] = flipped[0 : 2 * count, 0:modes_dev]
    cont_ref[...] = flipped[0 : 2 * count, modes_dev : 2 * modes_dev]


def local(sources, gauge_links, eigenvectors, elementals):
    slices, peers = lax.axis_size("tm"), lax.axis_size("space")
    _, _, _, _, nsrc, _, lanes = sources.shape
    nmode = eigenvectors.shape[1]
    modes_dev = elementals.shape[2]
    src = sources.transpose(0, 1, 3, 4, 5, 2, 6).reshape(24 * nsrc, lanes)
    link = gauge_links.transpose(0, 1, 3, 4, 5, 2, 6).reshape(72, lanes)
    vec = eigenvectors.transpose(0, 1, 3, 4, 2, 5).reshape(6 * nmode, lanes)
    elem = elementals.reshape(2, modes_dev, nmode)
    groups, half = nsrc // GROUP, 2 * GROUP
    halos = SWEEPS * groups * 4
    kind = bf16 if modes_dev % 16 == 0 else f32
    outs = jax.ShapeDtypeStruct((8 * nsrc, modes_dev), f32)
    dma = pltpu.SemaphoreType.DMA
    proj, cont = pl.pallas_call(
        functools.partial(kernel, slices, peers, nsrc, modes_dev),
        out_shape=(outs, outs),
        in_specs=[pl.BlockSpec(memory_space=pl.ANY)] * 4,
        out_specs=[pl.BlockSpec(memory_space=pltpu.VMEM)] * 2,
        scratch_shapes=[
            pltpu.VMEM(src.shape, bf16),
            pltpu.VMEM(link.shape, bf16),
            pltpu.VMEM(vec.shape, bf16),
            pltpu.VMEM(elem.shape, f32),
            dma((4,)),
            pltpu.VMEM(src.shape, f32),
            pltpu.VMEM(link.shape, f32),
            pltpu.VMEM((4, 2, 3, 3, half, lanes), f32),
            pltpu.VMEM((groups, 6, 2 * half, lanes), f32),
            pltpu.VMEM((groups, 6, 2 * half, lanes), f32),
            pltpu.VMEM((groups, 4, 3, half, lanes), f32),
            pltpu.VMEM(vec.shape, f32),
            pltpu.VMEM((halos, 6 * half, lanes), bf16),
            pltpu.VMEM((halos, 6 * half, lanes), bf16),
            dma((halos,)),
            dma((halos,)),
            pltpu.VMEM((peers, 2, modes_dev, nmode), kind),
            pltpu.VMEM((2, nmode, nmode), f32),
            dma((peers,)),
            dma((peers,)),
            pltpu.VMEM((2 * nmode, 6 * lanes), bf16),
            pltpu.VMEM((8 * nsrc, 6 * lanes), bf16),
            pltpu.VMEM((2 * nmode, 128), f32),
            pltpu.VMEM((peers, 2, modes_dev, 128), kind),
            pltpu.VMEM((peers, 2, modes_dev, 128), kind),
            dma((peers,)),
            dma((peers,)),
            pltpu.VMEM((128, 128), f32),
        ],
        compiler_params=pltpu.CompilerParams(
            collective_id=0, has_side_effects=True, vmem_limit_bytes=60 * 1024 * 1024
        ),
        cost_estimate=pl.CostEstimate(
            flops=200_000_000, bytes_accessed=1_000_000, transcendentals=0
        ),
    )(src, link, vec, elem)

    def placed(out):
        return out.reshape(1, 2, nsrc, 4, modes_dev).transpose(0, 1, 3, 2, 4)

    return placed(proj), placed(cont)


def solution(mesh):
    placed = (
        P("tm", None, None, None, None, "space", None),
        P(None, "tm", None, None, None, "space", None),
        P("tm", None, None, None, "space", None),
        P("tm", None, "space", None),
    )
    return jax.shard_map(
        local,
        mesh=mesh,
        in_specs=placed,
        out_specs=(P("tm", None, None, None, "space"), P("tm", None, None, None, "space")),
        check_vma=False,
    )
```

time: 29.6 us -> 27.4 us (0.926)
  local copies, waits for them, and re-layouts: 4.48 us -> 2.06 us
  Pallas kernels: 24.1 us -> 24.5 us
    unnamed x10 -> x4, local copies, waits for them, and re-layouts: 4.48 us -> 2.06 us
    pallas_call x1, Pallas kernels: 24.1 us -> 24.5 us  [local(): pl.pallas_call(functools.partial(kernel, slices, peers, nsrc, modes_dev),...]
where the time goes in v2:
time: 27.4 us; the launch traced here: 27.3 us
  Pallas kernels  24.5 us (89%)
  local copies, waits for them, and re-layouts  2.06 us (8%)
  between operations  0.65 us (2%)
    pallas_call x1, Pallas kernels, local(): pl.pallas_call(functools.partial(kernel, slices, peers, nsrc, modes_dev),...  24.5 us
    unnamed x4, local copies, waits for them, and re-layouts  2.06 us

profile of v2, /device:TPU:0, one launch (start us, length us, event | category | flops | bytes accessed | tf_op | source)
XLA Modules:
  0.0 27.3 jit_solution(32916703390686865)
XLA Ops:
  0.6 24.5 %shard_map.59 = (f32[96,16]{1,0:T(8,128)}, f32[96,16]{1,0:T(8,128)}) custom-call(bf16[288,128]{1,0:T(8,128)(2,1)} %bitcast.19, bf16[72,128]{1,0:T(8,128)(2,1)} %bitcast.20, bf16[768,128]{1,0:T(8,128)(2,1)} %bitcast.18, f32[2,16,128]{2,1,0:T(8,128)} %bitcast.21), custom_call_target="tpu_custom_call" | custom-call | flops 200000000 | bytes 1000000 | tf_op jit(solution)/shard_map/pallas_call | solution.py:348
  25.2 0.0 copy-start
  25.2 1.4 %copy.8 = f32[1,2,4,12,16]{4,2,3,1,0:T(4,128)} copy(f32[1,2,4,12,16]{4,2,3,1,0:T(4,128)} %bitcast.17) | data formatting | bytes 12288
  26.6 0.0 copy-done
  26.6 0.6 %copy.9 = f32[1,2,4,12,16]{4,2,3,1,0:T(4,128)} copy(f32[1,2,4,12,16]{4,2,3,1,0:T(4,128)S(1)} %bitcast.16) | data formatting | bytes 12288
Async XLA Ops:
  25.2 1.4 %copy-start = (f32[96,16]{1,0:T(8,128)S(1)}, f32[96,16]{1,0:T(8,128)}, u32[]{:S(2)}) copy-start(f32[96,16]{1,0:T(8,128)} %get-tuple-element.5) | copy-start | bytes 18436

commit v3 on v2

--- a/solution.py
+++ b/solution.py
@@ -27,12 +27,12 @@
 def kernel(
     slices, peers, nsrc, modes_dev,
     src_hbm, link_hbm, vec_hbm, elem_hbm,
-    proj_ref, cont_ref,
+    turned,
     src_in, link_in, vec_in, elem_in, load_sem,
     wide, link_wide, links, base, field, hops, vec_wide,
     halo_out, halo_in, halo_send, halo_recv,
     elem_all, elem_full, elem_send, elem_recv,
-    left_mat, right_mat, sums, part_out, part_in, part_send, part_recv, turned,
+    left_mat, right_mat, sums, part_out, part_in, part_send, part_recv,
 ):
     groups = nsrc // GROUP
     half = 2 * GROUP
@@ -152,17 +152,20 @@
     def turn_z(low):
         return spin_sign * low[1], -(spin_sign * low[0])
 
-    def send_minus(sweep, g):
+    def send_z(sweep, g, minus, plus):
         up, low = parts_of(g)
         turn = turn_z(low)
-        send(sweep, g, 2, (up[0] - turn[0], up[1] - turn[1]))
-        send(sweep, g, 0, (up[0] - low[0], up[1] - low[1]))
-
-    def send_plus(sweep, g):
+        if minus:
+            send(sweep, g, 2, (up[0] - turn[0], up[1] - turn[1]))
+        if plus:
+            send(sweep, g, 3, apply(2, (up[0] + turn[0], up[1] + turn[1]), True))
+
+    def send_t(sweep, g, minus, plus):
         up, low = parts_of(g)
-        turn = turn_z(low)
-        send(sweep, g, 3, apply(2, (up[0] + turn[0], up[1] + turn[1]), True))
-        send(sweep, g, 1, apply(3, (up[0] + low[0], up[1] + low[1]), True))
+        if minus:
+            send(sweep, g, 0, (up[0] - low[0], up[1] - low[1]))
+        if plus:
+            send(sweep, g, 1, apply(3, (up[0] + low[0], up[1] + low[1]), True))
 
     def plane(g):
         up, low = parts_of(g)
@@ -213,7 +216,9 @@
                 field[g, pc, spin * GROUP : (spin + 1) * GROUP, :] = piece
     pl.semaphore_wait(barrier, peers + 1)
     for g in range(groups):
-        send_minus(0, g)
+        send_z(0, g, True, False)
+    for g in range(groups):
+        send_t(0, g, True, False)
 
     loads[1].wait()
     link_wide[...] = link_in[...].astype(f32)
@@ -226,7 +231,9 @@
                         link_wide[row : row + 1, :], (half, lanes)
                     )
     for g in range(groups):
-        send_plus(0, g)
+        send_z(0, g, False, True)
+    for g in range(groups):
+        send_t(0, g, False, True)
 
     loads[2].wait()
     elem_all[me] = elem_in[...].astype(elem_all.dtype)
@@ -244,8 +251,8 @@
     for sweep in range(1, SWEEPS):
         for g in range(groups):
             finish(sweep - 1, g)
-            send_minus(sweep, g)
-            send_plus(sweep, g)
+            send_z(sweep, g, True, True)
+            send_t(sweep, g, True, True)
         for g in range(groups):
             plane(g)
         if sweep == 1:
@@ -326,9 +333,13 @@
             turned[o * modes_dev : (o + 1) * modes_dev, :] += part_in[p, o].astype(f32)
 
     each(1, peers, gather)
+
+
+def finish_kernel(turned, proj_ref, cont_ref):
+    count, modes_dev = proj_ref.shape
     flipped = turned[...].T
-    proj_ref[...] = flipped[0 : 2 * count, 0:modes_dev]
-    cont_ref[...] = flipped[0 : 2 * count, modes_dev : 2 * modes_dev]
+    proj_ref[...] = flipped[0:count, 0:modes_dev]
+    cont_ref[...] = flipped[0:count, modes_dev : 2 * modes_dev]
 
 
 def local(sources, gauge_links, eigenvectors, elementals):
@@ -342,14 +353,18 @@
     elem = elementals.reshape(2, modes_dev, nmode)
     groups, half = nsrc // GROUP, 2 * GROUP
     halos = SWEEPS * groups * 4
+    src, link, vec, elem = [
+        pltpu.with_memory_space_constraint(x, pltpu.HBM) for x in (src, link, vec, elem)
+    ]
     kind = bf16 if modes_dev % 16 == 0 else f32
     outs = jax.ShapeDtypeStruct((8 * nsrc, modes_dev), f32)
     dma = pltpu.SemaphoreType.DMA
-    proj, cont = pl.pallas_call(
+    vmem = pl.BlockSpec(memory_space=pltpu.VMEM)
+    turned = pl.pallas_call(
         functools.partial(kernel, slices, peers, nsrc, modes_dev),
-        out_shape=(outs, outs),
-        in_specs=[pl.BlockSpec(memory_space=pl.ANY)] * 4,
-        out_specs=[pl.BlockSpec(memory_space=pltpu.VMEM)] * 2,
+        out_shape=jax.ShapeDtypeStruct((128, 128), f32),
+        in_specs=[pl.BlockSpec(memory_space=pltpu.HBM)] * 4,
+        out_specs=vmem,
         scratch_shapes=[
             pltpu.VMEM(src.shape, bf16),
             pltpu.VMEM(link.shape, bf16),
@@ -378,15 +393,17 @@
             pltpu.VMEM((peers, 2, modes_dev, 128), kind),
             dma((peers,)),
             dma((peers,)),
-            pltpu.VMEM((128, 128), f32),
         ],
         compiler_params=pltpu.CompilerParams(
-            collective_id=0, has_side_effects=True, vmem_limit_bytes=60 * 1024 * 1024
+            collective_id=0, has_side_effects=True, vmem_limit_bytes=32 * 1024 * 1024
         ),
         cost_estimate=pl.CostEstimate(
             flops=200_000_000, bytes_accessed=1_000_000, transcendentals=0
         ),
     )(src, link, vec, elem)
+    proj, cont = pl.pallas_call(
+        finish_kernel, out_shape=(outs, outs), in_specs=[vmem], out_specs=[vmem] * 2
+    )(turned)
 
     def placed(out):
         return out.reshape(1, 2, nsrc, 4, modes_dev).transpose(0, 1, 3, 2, 4)

time: 27.4 us -> 26.9 us (0.982)
  local copies, waits for them, and re-layouts: 2.06 us -> 0.6 us
  Pallas kernels: 24.5 us -> 25.5 us
    pallas_call x0 -> x1, Pallas kernels: none -> 1.62 us  [local(): pl.pallas_call(finish_kernel, out_shape=(outs, outs), in_specs=[vmem], ou...]
    unnamed x4 -> x2, local copies, waits for them, and re-layouts: 2.06 us -> 0.6 us
    pallas_call x1, Pallas kernels: 24.5 us -> 23.9 us  [local(): pl.pallas_call(functools.partial(kernel, slices, peers, nsrc, modes_dev),...]
where the time goes in v3:
time: 26.9 us; the launch traced here: 26.7 us
  Pallas kernels  25.5 us (95%)
  between operations  0.65 us (2%)
  local copies, waits for them, and re-layouts  0.6 us (2%)
    pallas_call x1, Pallas kernels, local(): pl.pallas_call(functools.partial(kernel, slices, peers, nsrc, modes_dev),...  23.9 us
    pallas_call x1, Pallas kernels, local(): pl.pallas_call(finish_kernel, out_shape=(outs, outs), in_specs=[vmem], ou...  1.62 us
    unnamed x2, local copies, waits for them, and re-layouts  0.6 us

profile of v3, /device:TPU:0, one launch (start us, length us, event | category | flops | bytes accessed | tf_op | source)
XLA Modules:
  0.0 26.7 jit_solution(6147337482554635467)
XLA Ops:
  0.6 23.9 %shard_map.59.turned = f32[128,128]{1,0:T(8,128)S(1)} custom-call(bf16[288,128]{1,0:T(8,128)(2,1)} %bitcast.17, bf16[72,128]{1,0:T(8,128)(2,1)} %bitcast.20, bf16[768,128]{1,0:T(8,128)(2,1)} %bitcast.16, f32[2,16,128]{2,1,0:T(8,128)} %bitcast.21), custom_call_target="tpu_custom_call" | custom-call | flops 200000000 | bytes 1000000 | tf_op jit(solution)/shard_map/pallas_call | solution.py:363
  24.5 0.0 copy-start
  24.5 0.6 %copy-done = f32[128,128]{1,0:T(8,128)} copy-done((f32[128,128]{1,0:T(8,128)}, f32[128,128]{1,0:T(8,128)S(1)}, u32[]{:S(2)}) %copy-start) | copy-done | bytes 65560
  25.1 1.6 %shard_map.60 = (f32[96,16]{1,0:T(8,128)}, f32[96,16]{1,0:T(8,128)}) custom-call(f32[128,128]{1,0:T(8,128)} %copy-done), custom_call_target="tpu_custom_call" | custom-call | tf_op jit(solution)/shard_map/pallas_call | solution.py:404
Async XLA Ops:
  24.5 0.6 %copy-start = (f32[128,128]{1,0:T(8,128)}, f32[128,128]{1,0:T(8,128)S(1)}, u32[]{:S(2)}) copy-start(f32[128,128]{1,0:T(8,128)S(1)} %shard_map.59.turned) | copy-start | bytes 196612

commit v4 on v3

--- a/solution.py
+++ b/solution.py
@@ -27,12 +27,12 @@
 def kernel(
     slices, peers, nsrc, modes_dev,
     src_hbm, link_hbm, vec_hbm, elem_hbm,
-    turned,
+    proj_ref, cont_ref,
     src_in, link_in, vec_in, elem_in, load_sem,
     wide, link_wide, links, base, field, hops, vec_wide,
     halo_out, halo_in, halo_send, halo_recv,
     elem_all, elem_full, elem_send, elem_recv,
-    left_mat, right_mat, sums, part_out, part_in, part_send, part_recv,
+    left_mat, right_mat, sums, part_out, part_in, part_send, part_recv, turned,
 ):
     groups = nsrc // GROUP
     half = 2 * GROUP
@@ -288,20 +288,24 @@
                         nmode : 2 * nmode, (2 * c + part) * lanes : (2 * c + part + 1) * lanes
                     ] = mixed[part * nmode : (part + 1) * nmode]
 
+    count = 4 * nsrc
+    chunk = 4 * GROUP
     for g in range(groups):
         finish(SWEEPS - 1, g)
         for pc in range(6):
             for spin in range(4):
-                wide[pl.ds((pc * nsrc + g * GROUP) * 4 + spin, GROUP, stride=4), :] = field[
+                wide[pl.ds((g * 6 + pc) * chunk + spin, GROUP, stride=4), :] = field[
                     g, pc, spin * GROUP : (spin + 1) * GROUP, :
                 ]
-    count = 4 * nsrc
-    for c in range(3):
-        re = wide[c * count : (c + 1) * count, :]
-        im = wide[(3 + c) * count : (4 + c) * count, :]
-        at = 2 * c * lanes
-        right_mat[:, at : at + lanes] = jnp.concatenate([re, im], 0).astype(bf16)
-        right_mat[:, at + lanes : at + 2 * lanes] = jnp.concatenate([im, -re], 0).astype(bf16)
+        rows = slice(2 * g * chunk, 2 * (g + 1) * chunk)
+        for c in range(3):
+            re_at, im_at = (g * 6 + c) * chunk, (g * 6 + 3 + c) * chunk
+            re, im = wide[re_at : re_at + chunk, :], wide[im_at : im_at + chunk, :]
+            at = 2 * c * lanes
+            right_mat[rows, at : at + lanes] = jnp.concatenate([re, im], 0).astype(bf16)
+            right_mat[rows, at + lanes : at + 2 * lanes] = jnp.concatenate(
+                [im, -re], 0
+            ).astype(bf16)
     sums[:, 0 : 2 * count] = lax.dot_general(
         left_mat[...], right_mat[...], (((1,), (1,)), ((), ())), preferred_element_type=f32
     )
@@ -333,13 +337,13 @@
             turned[o * modes_dev : (o + 1) * modes_dev, :] += part_in[p, o].astype(f32)
 
     each(1, peers, gather)
-
-
-def finish_kernel(turned, proj_ref, cont_ref):
-    count, modes_dev = proj_ref.shape
     flipped = turned[...].T
-    proj_ref[...] = flipped[0:count, 0:modes_dev]
-    cont_ref[...] = flipped[0:count, modes_dev : 2 * modes_dev]
+    for g in range(groups):
+        for part in range(2):
+            got = flipped[(2 * g + part) * chunk : (2 * g + part + 1) * chunk]
+            to = slice(part * count + g * chunk, part * count + (g + 1) * chunk)
+            proj_ref[to, :] = got[:, 0:modes_dev]
+            cont_ref[to, :] = got[:, modes_dev : 2 * modes_dev]
 
 
 def local(sources, gauge_links, eigenvectors, elementals):
@@ -360,11 +364,11 @@
     outs = jax.ShapeDtypeStruct((8 * nsrc, modes_dev), f32)
     dma = pltpu.SemaphoreType.DMA
     vmem = pl.BlockSpec(memory_space=pltpu.VMEM)
-    turned = pl.pallas_call(
+    proj, cont = pl.pallas_call(
         functools.partial(kernel, slices, peers, nsrc, modes_dev),
-        out_shape=jax.ShapeDtypeStruct((128, 128), f32),
+        out_shape=(outs, outs),
         in_specs=[pl.BlockSpec(memory_space=pltpu.HBM)] * 4,
-        out_specs=vmem,
+        out_specs=[vmem] * 2,
         scratch_shapes=[
             pltpu.VMEM(src.shape, bf16),
             pltpu.VMEM(link.shape, bf16),
@@ -393,6 +397,7 @@
             pltpu.VMEM((peers, 2, modes_dev, 128), kind),
             dma((peers,)),
             dma((peers,)),
+            pltpu.VMEM((128, 128), f32),
         ],
         compiler_params=pltpu.CompilerParams(
             collective_id=0, has_side_effects=True, vmem_limit_bytes=32 * 1024 * 1024
@@ -401,9 +406,6 @@
             flops=200_000_000, bytes_accessed=1_000_000, transcendentals=0
         ),
     )(src, link, vec, elem)
-    proj, cont = pl.pallas_call(
-        finish_kernel, out_shape=(outs, outs), in_specs=[vmem], out_specs=[vmem] * 2
-    )(turned)
 
     def placed(out):
         return out.reshape(1, 2, nsrc, 4, modes_dev).transpose(0, 1, 3, 2, 4)

time: 26.9 us -> 26 us (0.967)
  Pallas kernels: 25.5 us -> 24 us
  local copies, waits for them, and re-layouts: 0.6 us -> 1.24 us
    pallas_call x1 -> x0, Pallas kernels: 1.62 us -> none  [local(): pl.pallas_call(finish_kernel, out_shape=(outs, outs), in_specs=[vmem], ou...]
    unnamed x2, local copies, waits for them, and re-layouts: 0.6 us -> 1.24 us
where the time goes in v4:
time: 26 us; the launch traced here: 25.9 us
  Pallas kernels  24 us (92%)
  local copies, waits for them, and re-layouts  1.24 us (5%)
  between operations  0.64 us (2%)
    pallas_call x1, Pallas kernels, local(): pl.pallas_call(functools.partial(kernel, slices, peers, nsrc, modes_dev),...  24 us
    unnamed x2, local copies, waits for them, and re-layouts  1.24 us

profile of v4, /device:TPU:0, one launch (start us, length us, event | category | flops | bytes accessed | tf_op | source)
XLA Modules:
  0.0 25.9 jit_solution(14725621649784005442)
XLA Ops:
  0.6 24.0 %shard_map.59 = (f32[96,16]{1,0:T(8,128)S(1)}, f32[96,16]{1,0:T(8,128)S(1)}) custom-call(bf16[288,128]{1,0:T(8,128)(2,1)} %bitcast.19, bf16[72,128]{1,0:T(8,128)(2,1)} %bitcast.20, bf16[768,128]{1,0:T(8,128)(2,1)} %bitcast.18, f32[2,16,128]{2,1,0:T(8,128)} %bitcast.21), custom_call_target="tpu_custom_call" | custom-call | flops 200000000 | bytes 1000000 | tf_op jit(solution)/shard_map/pallas_call | solution.py:367
  24.6 0.6 %copy.8 = f32[1,2,4,12,16]{4,2,3,1,0:T(4,128)} copy(f32[1,2,4,12,16]{4,2,3,1,0:T(4,128)S(1)} %bitcast.17) | data formatting | bytes 12288
  25.3 0.6 %copy.9 = f32[1,2,4,12,16]{4,2,3,1,0:T(4,128)} copy(f32[1,2,4,12,16]{4,2,3,1,0:T(4,128)S(1)} %bitcast.16) | data formatting | bytes 12288

commit v5 on v4

--- a/solution.py
+++ b/solution.py
@@ -17,11 +17,11 @@
 
 
 def each(lower, upper, body):
-    if upper - lower <= 16:
-        for index in range(lower, upper):
-            body(index)
-    else:
-        lax.fori_loop(lower, upper, lambda index, carry: (body(index), carry)[1], 0)
+    lax.fori_loop(lower, upper, lambda index, carry: (body(index), carry)[1], 0)
+
+
+def loop(count, body):
+    each(0, count, body)
 
 
 def kernel(
@@ -45,15 +45,6 @@
 
     barrier = pltpu.get_barrier_semaphore()
 
-    def greet(off):
-        pl.semaphore_signal(
-            barrier, inc=1, device_id=(t, lax.rem(me + off, peers)), device_id_type=MESH
-        )
-
-    for near in (t_up, t_down):
-        pl.semaphore_signal(barrier, inc=1, device_id=(near, me), device_id_type=MESH)
-    each(1, peers, greet)
-
     loads = [
         pltpu.make_async_copy(a, b, load_sem.at[i])
         for i, (a, b) in enumerate(
@@ -62,6 +53,15 @@
     ]
     for load in loads:
         load.start()
+
+    def greet(off):
+        pl.semaphore_signal(
+            barrier, inc=1, device_id=(t, lax.rem(me + off, peers)), device_id_type=MESH
+        )
+
+    for near in (t_up, t_down):
+        pl.semaphore_signal(barrier, inc=1, device_id=(near, me), device_id_type=MESH)
+    each(1, peers, greet)
 
     row_at = lax.broadcasted_iota(jnp.int32, (1, half, lanes), 1)
     spin_sign = jnp.where(row_at < GROUP, 1.0, -1.0).astype(f32)
@@ -206,23 +206,9 @@
             field[g, at, 0:half, :] = new_up.astype(bf16).astype(f32)
             field[g, at, half : 2 * half, :] = new_low.astype(bf16).astype(f32)
 
-    loads[0].wait()
-    wide[...] = src_in[...].astype(f32)
-    for g in range(groups):
-        for pc in range(6):
-            for spin in range(4):
-                piece = wide[pl.ds((pc * nsrc + g * GROUP) * 4 + spin, GROUP, stride=4), :]
-                base[g, pc, spin * GROUP : (spin + 1) * GROUP, :] = piece
-                field[g, pc, spin * GROUP : (spin + 1) * GROUP, :] = piece
-    pl.semaphore_wait(barrier, peers + 1)
-    for g in range(groups):
-        send_z(0, g, True, False)
-    for g in range(groups):
-        send_t(0, g, True, False)
-
     loads[1].wait()
     link_wide[...] = link_in[...].astype(f32)
-    for mu in (2, 3, 0, 1):
+    for mu in range(4):
         for i in range(3):
             for j in range(3):
                 for part in range(2):
@@ -230,82 +216,103 @@
                     links[mu, part, i, j] = jnp.broadcast_to(
                         link_wide[row : row + 1, :], (half, lanes)
                     )
-    for g in range(groups):
-        send_z(0, g, False, True)
-    for g in range(groups):
-        send_t(0, g, False, True)
-
-    loads[2].wait()
-    elem_all[me] = elem_in[...].astype(elem_all.dtype)
-    each(1, peers, lambda off: elem_copy(lax.rem(me + off, peers), me).start())
-    for g in range(groups):
-        plane(g)
-
-    loads[3].wait()
-    vec_wide[...] = vec_in[...].astype(f32)
-    for j in range(6):
-        left_mat[0:nmode, j * lanes : (j + 1) * lanes] = vec_wide[
-            pl.ds(j, nmode, stride=6), :
-        ].astype(bf16)
-
-    for sweep in range(1, SWEEPS):
-        for g in range(groups):
-            finish(sweep - 1, g)
-            send_z(sweep, g, True, True)
-            send_t(sweep, g, True, True)
-        for g in range(groups):
-            plane(g)
-        if sweep == 1:
-            def arrive(off):
-                p = lax.rem(me + off, peers)
-                elem_copy(p, p).wait_recv()
-
-            each(1, peers, arrive)
-            for p in range(peers):
-                for part in range(2):
-                    elem_full[part, p * modes_dev : (p + 1) * modes_dev, :] = elem_all[
-                        p, part
-                    ].astype(f32)
-            e_re, e_im = elem_full[0].astype(bf16), elem_full[1].astype(bf16)
-            blocks = jnp.concatenate(
+
+    loads[0].wait()
+    wide[...] = src_in[...].astype(f32)
+
+    def arrange(g):
+        for pc in range(6):
+            for spin in range(4):
+                piece = wide[pl.ds((pc * nsrc + g * GROUP) * 4 + spin, GROUP, stride=4), :]
+                base[g, pc, spin * GROUP : (spin + 1) * GROUP, :] = piece
+                field[g, pc, spin * GROUP : (spin + 1) * GROUP, :] = piece
+
+    loop(groups, arrange)
+    pl.semaphore_wait(barrier, peers + 1)
+
+    def spread():
+        loads[2].wait()
+        elem_all[me] = elem_in[...].astype(elem_all.dtype)
+        each(1, peers, lambda off: elem_copy(lax.rem(me + off, peers), me).start())
+        loads[3].wait()
+        vec_wide[...] = vec_in[...].astype(f32)
+        for j in range(6):
+            left_mat[0:nmode, j * lanes : (j + 1) * lanes] = vec_wide[
+                pl.ds(j, nmode, stride=6), :
+            ].astype(bf16)
+
+    def mix():
+        def arrive(off):
+            p = lax.rem(me + off, peers)
+            elem_copy(p, p).wait_recv()
+
+        each(1, peers, arrive)
+        for p in range(peers):
+            for part in range(2):
+                elem_full[part, p * modes_dev : (p + 1) * modes_dev, :] = elem_all[
+                    p, part
+                ].astype(f32)
+        e_re, e_im = elem_full[0].astype(bf16), elem_full[1].astype(bf16)
+        blocks = jnp.concatenate(
+            [
+                jnp.concatenate([e_re, e_im], 1),
+                jnp.concatenate([-e_im, e_re], 1),
+            ],
+            0,
+        )
+        for c in range(3):
+            both = jnp.concatenate(
                 [
-                    jnp.concatenate([e_re, e_im], 1),
-                    jnp.concatenate([-e_im, e_re], 1),
+                    left_mat[0:nmode, (2 * c + part) * lanes : (2 * c + part + 1) * lanes]
+                    for part in range(2)
                 ],
                 0,
             )
-            for c in range(3):
-                both = jnp.concatenate(
-                    [
-                        left_mat[0:nmode, (2 * c + part) * lanes : (2 * c + part + 1) * lanes]
-                        for part in range(2)
-                    ],
-                    0,
-                )
-                mixed = jnp.dot(blocks, both, preferred_element_type=f32).astype(bf16)
-                for part in range(2):
-                    left_mat[
-                        nmode : 2 * nmode, (2 * c + part) * lanes : (2 * c + part + 1) * lanes
-                    ] = mixed[part * nmode : (part + 1) * nmode]
+            mixed = jnp.dot(blocks, both, preferred_element_type=f32).astype(bf16)
+            for part in range(2):
+                left_mat[
+                    nmode : 2 * nmode, (2 * c + part) * lanes : (2 * c + part + 1) * lanes
+                ] = mixed[part * nmode : (part + 1) * nmode]
+
+    def step(sweep):
+        def group(g):
+            @pl.when(sweep > 0)
+            def _():
+                finish(sweep - 1, g)
+
+            send_z(sweep, g, True, True)
+            send_t(sweep, g, True, True)
+
+        loop(groups, group)
+        pl.when(sweep == 0)(spread)
+        loop(groups, plane)
+        pl.when(sweep == 1)(mix)
+
+    loop(SWEEPS, step)
 
     count = 4 * nsrc
     chunk = 4 * GROUP
-    for g in range(groups):
+
+    def close(g):
         finish(SWEEPS - 1, g)
         for pc in range(6):
             for spin in range(4):
                 wide[pl.ds((g * 6 + pc) * chunk + spin, GROUP, stride=4), :] = field[
                     g, pc, spin * GROUP : (spin + 1) * GROUP, :
                 ]
-        rows = slice(2 * g * chunk, 2 * (g + 1) * chunk)
+        rows = pl.ds(pl.multiple_of(2 * g * chunk, 2 * chunk), 2 * chunk)
         for c in range(3):
-            re_at, im_at = (g * 6 + c) * chunk, (g * 6 + 3 + c) * chunk
-            re, im = wide[re_at : re_at + chunk, :], wide[im_at : im_at + chunk, :]
+            re_at, im_at = [
+                pl.multiple_of((g * 6 + 3 * part + c) * chunk, chunk) for part in range(2)
+            ]
+            re, im = wide[pl.ds(re_at, chunk), :], wide[pl.ds(im_at, chunk), :]
             at = 2 * c * lanes
             right_mat[rows, at : at + lanes] = jnp.concatenate([re, im], 0).astype(bf16)
             right_mat[rows, at + lanes : at + 2 * lanes] = jnp.concatenate(
                 [im, -re], 0
             ).astype(bf16)
+
+    loop(groups, close)
     sums[:, 0 : 2 * count] = lax.dot_general(
         left_mat[...], right_mat[...], (((1,), (1,)), ((), ())), preferred_element_type=f32
     )
@@ -324,10 +331,11 @@
         elem_copy(p, me).wait_send()
         part_copy(p, me).wait_send()
 
-    for sweep in range(SWEEPS):
-        for g in range(groups):
-            for way in range(4):
-                halo(sweep, g, way).wait_send()
+    def settle_group(index):
+        for way in range(4):
+            halo(0, index, way).wait_send()
+
+    loop(SWEEPS * groups, settle_group)
     each(1, peers, settle)
 
     def gather(off):

time: 26 us -> 26.1 us (level)
  no operation moved by 1% of the time
where the time goes in v5:
time: 26.1 us; the launch traced here: 25.9 us
  Pallas kernels  24.1 us (92%)
  local copies, waits for them, and re-layouts  1.24 us (5%)
  between operations  0.64 us (2%)
    pallas_call x1, Pallas kernels, local(): pl.pallas_call(functools.partial(kernel, slices, peers, nsrc, modes_dev),...  24.1 us
    unnamed x2, local copies, waits for them, and re-layouts  1.24 us

profile of v5, /device:TPU:0, one launch (start us, length us, event | category | flops | bytes accessed | tf_op | source)
XLA Modules:
  0.0 25.9 jit_solution(12328622457911598316)
XLA Ops:
  0.6 24.1 %shard_map.59 = (f32[96,16]{1,0:T(8,128)S(1)}, f32[96,16]{1,0:T(8,128)S(1)}) custom-call(bf16[288,128]{1,0:T(8,128)(2,1)} %bitcast.19, bf16[72,128]{1,0:T(8,128)(2,1)} %bitcast.20, bf16[768,128]{1,0:T(8,128)(2,1)} %bitcast.18, f32[2,16,128]{2,1,0:T(8,128)} %bitcast.21), custom_call_target="tpu_custom_call" | custom-call | flops 200000000 | bytes 1000000 | tf_op jit(solution)/shard_map/pallas_call | solution.py:375
  24.7 0.6 %copy.8 = f32[1,2,4,12,16]{4,2,3,1,0:T(4,128)} copy(f32[1,2,4,12,16]{4,2,3,1,0:T(4,128)S(1)} %bitcast.17) | data formatting | bytes 12288
  25.3 0.6 %copy.9 = f32[1,2,4,12,16]{4,2,3,1,0:T(4,128)} copy(f32[1,2,4,12,16]{4,2,3,1,0:T(4,128)S(1)} %bitcast.16) | data formatting | bytes 12288

commit v6 on v5

--- a/solution.py
+++ b/solution.py
@@ -134,12 +134,12 @@
             device_id_type=MESH,
         )
 
-    def part_copy(to, slot):
+    def part_copy(wave, to, slot):
         return pltpu.make_async_remote_copy(
-            src_ref=part_out.at[to],
-            dst_ref=part_in.at[slot],
-            send_sem=part_send.at[to],
-            recv_sem=part_recv.at[slot],
+            src_ref=part_out.at[wave, to],
+            dst_ref=part_in.at[wave, slot],
+            send_sem=part_send.at[wave * peers + to],
+            recv_sem=part_recv.at[wave * peers + slot],
             device_id=(t, to),
             device_id_type=MESH,
         )
@@ -312,24 +312,40 @@
                 [im, -re], 0
             ).astype(bf16)
 
-    loop(groups, close)
-    sums[:, 0 : 2 * count] = lax.dot_general(
-        left_mat[...], right_mat[...], (((1,), (1,)), ((), ())), preferred_element_type=f32
-    )
-    for p in range(peers):
+    early = groups - 1
+    waves = ((0, early), (early, groups))
+    mid = sums.shape[-1] // 2
+
+    def emit(wave):
+        first, last = waves[wave]
+        right = right_mat[2 * first * chunk : 2 * last * chunk, :]
+        width = 2 * (last - first) * chunk
         for o in range(2):
-            at = o * nmode + p * modes_dev
-            part_out[p, o] = sums[at : at + modes_dev, :].astype(part_out.dtype)
-    each(1, peers, lambda off: part_copy(lax.rem(me + off, peers), me).start())
+            sums[wave, :, o * mid : o * mid + width] = lax.dot_general(
+                left_mat[o * nmode : (o + 1) * nmode, :],
+                right,
+                (((1,), (1,)), ((), ())),
+                preferred_element_type=f32,
+            )
+        for p in range(peers):
+            part_out[wave, p] = sums[wave, p * modes_dev : (p + 1) * modes_dev, :].astype(
+                part_out.dtype
+            )
+        each(1, peers, lambda off: part_copy(wave, lax.rem(me + off, peers), me).start())
+
+    for wave in range(2):
+        each(*waves[wave], close)
+        emit(wave)
 
     turned[...] = jnp.zeros_like(turned)
-    for o in range(2):
-        turned[o * modes_dev : (o + 1) * modes_dev, :] = part_out[me, o].astype(f32)
+    for wave in range(2):
+        turned[wave * modes_dev : (wave + 1) * modes_dev, :] = part_out[wave, me].astype(f32)
 
     def settle(off):
         p = lax.rem(me + off, peers)
         elem_copy(p, me).wait_send()
-        part_copy(p, me).wait_send()
+        for wave in range(2):
+            part_copy(wave, p, me).wait_send()
 
     def settle_group(index):
         for way in range(4):
@@ -338,20 +354,23 @@
     loop(SWEEPS * groups, settle_group)
     each(1, peers, settle)
 
-    def gather(off):
-        p = lax.rem(me + off, peers)
-        part_copy(p, p).wait_recv()
-        for o in range(2):
-            turned[o * modes_dev : (o + 1) * modes_dev, :] += part_in[p, o].astype(f32)
-
-    each(1, peers, gather)
+    for wave in range(2):
+
+        def gather(off):
+            p = lax.rem(me + off, peers)
+            part_copy(wave, p, p).wait_recv()
+            turned[wave * modes_dev : (wave + 1) * modes_dev, :] += part_in[wave, p].astype(f32)
+
+        each(1, peers, gather)
     flipped = turned[...].T
     for g in range(groups):
+        wave = 1 if g == early else 0
         for part in range(2):
-            got = flipped[(2 * g + part) * chunk : (2 * g + part + 1) * chunk]
+            row = (2 * (g - waves[wave][0]) + part) * chunk
+            cols = slice(wave * modes_dev, (wave + 1) * modes_dev)
             to = slice(part * count + g * chunk, part * count + (g + 1) * chunk)
-            proj_ref[to, :] = got[:, 0:modes_dev]
-            cont_ref[to, :] = got[:, modes_dev : 2 * modes_dev]
+            proj_ref[to, :] = flipped[row : row + chunk, cols]
+            cont_ref[to, :] = flipped[mid + row : mid + row + chunk, cols]
 
 
 def local(sources, gauge_links, eigenvectors, elementals):
@@ -400,11 +419,11 @@
             dma((peers,)),
             pltpu.VMEM((2 * nmode, 6 * lanes), bf16),
             pltpu.VMEM((8 * nsrc, 6 * lanes), bf16),
-            pltpu.VMEM((2 * nmode, 128), f32),
-            pltpu.VMEM((peers, 2, modes_dev, 128), kind),
-            pltpu.VMEM((peers, 2, modes_dev, 128), kind),
-            dma((peers,)),
-            dma((peers,)),
+            pltpu.VMEM((2, nmode, 128), f32),
+            pltpu.VMEM((2, peers, modes_dev, 128), kind),
+            pltpu.VMEM((2, peers, modes_dev, 128), kind),
+            dma((2 * peers,)),
+            dma((2 * peers,)),
             pltpu.VMEM((128, 128), f32),
         ],
         compiler_params=pltpu.CompilerParams(

time: 26.1 us -> 26.5 us (1.015)
  Pallas kernels: 24.1 us -> 24.4 us
    pallas_call x1, Pallas kernels: 24.1 us -> 24.4 us  [local(): pl.pallas_call(functools.partial(kernel, slices, peers, nsrc, modes_dev),...]
where the time goes in v6:
time: 26.5 us; the launch traced here: 26.3 us
  Pallas kernels  24.4 us (92%)
  local copies, waits for them, and re-layouts  1.24 us (5%)
  between operations  0.64 us (2%)
    pallas_call x1, Pallas kernels, local(): pl.pallas_call(functools.partial(kernel, slices, peers, nsrc, modes_dev),...  24.4 us
    unnamed x2, local copies, waits for them, and re-layouts  1.24 us

profile of v6, /device:TPU:0, one launch (start us, length us, event | category | flops | bytes accessed | tf_op | source)
XLA Modules:
  0.0 26.3 jit_solution(13905147522392181341)
XLA Ops:
  0.6 24.4 %shard_map.59 = (f32[96,16]{1,0:T(8,128)S(1)}, f32[96,16]{1,0:T(8,128)S(1)}) custom-call(bf16[288,128]{1,0:T(8,128)(2,1)} %bitcast.19, bf16[72,128]{1,0:T(8,128)(2,1)} %bitcast.20, bf16[768,128]{1,0:T(8,128)(2,1)} %bitcast.18, f32[2,16,128]{2,1,0:T(8,128)} %bitcast.21), custom_call_target="tpu_custom_call" | custom-call | flops 200000000 | bytes 1000000 | tf_op jit(solution)/shard_map/pallas_call | solution.py:394
  25.1 0.6 %copy.8 = f32[1,2,4,12,16]{4,2,3,1,0:T(4,128)} copy(f32[1,2,4,12,16]{4,2,3,1,0:T(4,128)S(1)} %bitcast.17) | data formatting | bytes 12288
  25.7 0.6 %copy.9 = f32[1,2,4,12,16]{4,2,3,1,0:T(4,128)} copy(f32[1,2,4,12,16]{4,2,3,1,0:T(4,128)S(1)} %bitcast.16) | data formatting | bytes 12288

commit v7 on v5

--- a/solution.py
+++ b/solution.py
@@ -281,9 +281,9 @@
                 finish(sweep - 1, g)
 
             send_z(sweep, g, True, True)
-            send_t(sweep, g, True, True)
 
         loop(groups, group)
+        loop(groups, lambda g: send_t(sweep, g, True, True))
         pl.when(sweep == 0)(spread)
         loop(groups, plane)
         pl.when(sweep == 1)(mix)

time: 26.1 us -> 26 us (level)
  no operation moved by 1% of the time
where the time goes in v7:
time: 26 us; the launch traced here: 25.8 us
  Pallas kernels  24 us (92%)
  local copies, waits for them, and re-layouts  1.24 us (5%)
  between operations  0.64 us (2%)
    pallas_call x1, Pallas kernels, local(): pl.pallas_call(functools.partial(kernel, slices, peers, nsrc, modes_dev),...  24 us
    unnamed x2, local copies, waits for them, and re-layouts  1.24 us

profile of v7, /device:TPU:0, one launch (start us, length us, event | category | flops | bytes accessed | tf_op | source)
XLA Modules:
  0.0 25.8 jit_solution(14302561156936590832)
XLA Ops:
  0.6 24.0 %shard_map.59 = (f32[96,16]{1,0:T(8,128)S(1)}, f32[96,16]{1,0:T(8,128)S(1)}) custom-call(bf16[288,128]{1,0:T(8,128)(2,1)} %bitcast.19, bf16[72,128]{1,0:T(8,128)(2,1)} %bitcast.20, bf16[768,128]{1,0:T(8,128)(2,1)} %bitcast.18, f32[2,16,128]{2,1,0:T(8,128)} %bitcast.21), custom_call_target="tpu_custom_call" | custom-call | flops 200000000 | bytes 1000000 | tf_op jit(solution)/shard_map/pallas_call | solution.py:375
  24.6 0.6 %copy.8 = f32[1,2,4,12,16]{4,2,3,1,0:T(4,128)} copy(f32[1,2,4,12,16]{4,2,3,1,0:T(4,128)S(1)} %bitcast.17) | data formatting | bytes 12288
  25.2 0.6 %copy.9 = f32[1,2,4,12,16]{4,2,3,1,0:T(4,128)} copy(f32[1,2,4,12,16]{4,2,3,1,0:T(4,128)S(1)} %bitcast.16) | data formatting | bytes 12288

commit v8 on v7

--- a/solution.py
+++ b/solution.py
@@ -105,11 +105,13 @@
         return value[:3], value[3:]
 
     def halo(sweep, g, way):
-        at = (sweep * groups + g) * 4 + way
+        first = (sweep * 4 + way) * groups
+        at = first if way < 2 else first + g
+        block = pl.ds(first, groups) if way < 2 else at
         target = ((t_down, me), (t_up, me), (t, z_down), (t, z_up))[way]
         return pltpu.make_async_remote_copy(
-            src_ref=halo_out.at[at],
-            dst_ref=halo_in.at[at],
+            src_ref=halo_out.at[block],
+            dst_ref=halo_in.at[block],
             send_sem=halo_send.at[at],
             recv_sem=halo_recv.at[at],
             device_id=target,
@@ -117,12 +119,16 @@
         )
 
     def send(sweep, g, way, pair):
-        halo_out[(sweep * groups + g) * 4 + way] = packed(pair)
-        halo(sweep, g, way).start()
+        halo_out[(sweep * 4 + way) * groups + g] = packed(pair)
+        if way >= 2:
+            halo(sweep, g, way).start()
 
     def receive(sweep, g, way):
-        halo(sweep, g, way).wait_recv()
-        return unpacked(halo_in[(sweep * groups + g) * 4 + way])
+        if way < 2:
+            pl.when(g == 0)(lambda: halo(sweep, g, way).wait_recv())
+        else:
+            halo(sweep, g, way).wait_recv()
+        return unpacked(halo_in[(sweep * 4 + way) * groups + g])
 
     def elem_copy(to, slot):
         return pltpu.make_async_remote_copy(
@@ -283,7 +289,9 @@
             send_z(sweep, g, True, True)
 
         loop(groups, group)
-        loop(groups, lambda g: send_t(sweep, g, True, True))
+        for way in range(2):
+            loop(groups, lambda g: send_t(sweep, g, way == 0, way == 1))
+            halo(sweep, 0, way).start()
         pl.when(sweep == 0)(spread)
         loop(groups, plane)
         pl.when(sweep == 1)(mix)
@@ -331,11 +339,11 @@
         elem_copy(p, me).wait_send()
         part_copy(p, me).wait_send()
 
-    def settle_group(index):
+    def settle_sweep(sweep):
         for way in range(4):
-            halo(0, index, way).wait_send()
-
-    loop(SWEEPS * groups, settle_group)
+            each(0, 1 if way < 2 else groups, lambda g: halo(sweep, g, way).wait_send())
+
+    loop(SWEEPS, settle_sweep)
     each(1, peers, settle)
 
     def gather(off):

time: 26 us -> 26 us (level)
  no operation moved by 1% of the time
where the time goes in v8:
time: 26 us; the launch traced here: 25.8 us
  Pallas kernels  23.9 us (92%)
  local copies, waits for them, and re-layouts  1.24 us (5%)
  between operations  0.64 us (2%)
    pallas_call x1, Pallas kernels, local(): pl.pallas_call(functools.partial(kernel, slices, peers, nsrc, modes_dev),...  23.9 us
    unnamed x2, local copies, waits for them, and re-layouts  1.24 us

profile of v8, /device:TPU:0, one launch (start us, length us, event | category | flops | bytes accessed | tf_op | source)
XLA Modules:
  0.0 25.8 jit_solution(10454983141013775018)
XLA Ops:
  0.6 23.9 %shard_map.59 = (f32[96,16]{1,0:T(8,128)S(1)}, f32[96,16]{1,0:T(8,128)S(1)}) custom-call(bf16[288,128]{1,0:T(8,128)(2,1)} %bitcast.19, bf16[72,128]{1,0:T(8,128)(2,1)} %bitcast.20, bf16[768,128]{1,0:T(8,128)(2,1)} %bitcast.18, f32[2,16,128]{2,1,0:T(8,128)} %bitcast.21), custom_call_target="tpu_custom_call" | custom-call | flops 200000000 | bytes 1000000 | tf_op jit(solution)/shard_map/pallas_call | solution.py:383
  24.6 0.6 %copy.8 = f32[1,2,4,12,16]{4,2,3,1,0:T(4,128)} copy(f32[1,2,4,12,16]{4,2,3,1,0:T(4,128)S(1)} %bitcast.17) | data formatting | bytes 12288
  25.2 0.6 %copy.9 = f32[1,2,4,12,16]{4,2,3,1,0:T(4,128)} copy(f32[1,2,4,12,16]{4,2,3,1,0:T(4,128)S(1)} %bitcast.16) | data formatting | bytes 12288
